TPU v7x, 32 devices: a whole 2x2x4 slice. The times are simulated.
32 devices in a mesh: groups: 2 (over x), bunch: 8 (over z, y), pencil: 2 (over core).
Axes of the slice: x: 2, y: 2, z: 4, core: 2. Of those that a mesh axis runs over, the one named last changes fastest.
Arguments:
- charge: bfloat16 [16, 32768], P(('groups', 'bunch'), 'pencil'), parts along dimension 0, may hold values from 0.25 to 4
- cell_deposit: int32 [16, 32768], P(('groups', 'bunch'), 'pencil'), parts along dimension 0, may hold values from 0 to 65535
- cell_gather: int32 [16, 32768], P(('groups', 'bunch'), 'pencil'), parts along dimension 0, may hold values from 0 to 65535
- green_spectra: float32 [7, 2, 64, 64, 128], P(None, None, None, 'pencil'), may hold values from -6 to 6
Outputs:
- field_at_particles: float32 [3, 16, 32768], P(None, ('groups', 'bunch'), 'pencil'), parts along dimension 1
There are 2 independent parts, one for each index of `groups`. A program takes and returns all parts, laid end to end along the dimension named above; an argument that names none is the same for every part. Nothing has to cross between parts.
Inputs may be any that keep to these rules, and one draw needn't show every extreme that they name: `cell_deposit`: flat cell index (x * 32 + y) * 64 + z. `cell_gather`: flat cell index (x * 32 + y) * 64 + z.
All inputs are finite; a program needn't handle non-finite values.
Results may differ from a plain program's by a relative error of at most 0.0029.
Values may be sent and summed in bfloat16 or wider, within the bound.
No kernel may reach another device: no remote copies, remote signals or barrier semaphores. Data moves between devices by JAX's collectives and lax.ppermute only.
A program may use at most 128 MiB of HBM per device.

v0:
```python
import functools

import jax
import jax.numpy as jnp
import numpy as np
from jax import lax
from jax.experimental import pallas as pl
from jax.experimental.pallas import tpu as pltpu
from jax.sharding import PartitionSpec as P

GX = 32
GY = 32
GZ = 64
SPAN = 3
MX = 64
MY = 64
MZ = 128
BF16 = jnp.bfloat16
F32 = jnp.float32
DEPOSIT_BLOCK = 2048
GATHER_BLOCK = 1024


def hi_lo(table):
    top = table.astype(np.float32).astype(BF16)
    rest = (table - top.astype(np.float64)).astype(np.float32).astype(BF16)
    return top, rest


def stacked_terms(table):
    top, rest = hi_lo(table)
    return np.concatenate([top, top, rest], axis=-1)


def phases(rows, columns, period):
    angles = 2.0 * np.pi / period * ((rows[:, None] * columns[None, :]) % period)
    return np.cos(angles), np.sin(angles)


def make_tables(pencils):
    width = MY // pencils
    cos_z, sin_z = phases(np.arange(GZ), np.arange(MZ), MZ)
    piece = np.concatenate([cos_z, -sin_z], axis=1)
    forward_z = np.kron(np.eye(4), piece)
    grid_x = (np.arange(8)[None, :] * 4 + np.arange(4)[:, None]).reshape(-1)
    cos_x, sin_x = phases(np.arange(MX), grid_x, MX)
    forward_x = np.block([[cos_x, sin_x], [-sin_x, cos_x]])
    forward_y = []
    inverse_y = []
    for pencil in range(pencils):
        own = np.arange(pencil * width, (pencil + 1) * width)
        cos_y, sin_y = phases(own, np.arange(GY), MY)
        forward_y.append(stacked_terms(np.block([[cos_y, sin_y], [-sin_y, cos_y]])))
        inverse_y.append(stacked_terms(np.concatenate([cos_y.T, sin_y.T], axis=0)))
    cos_b, sin_b = phases(np.arange(MZ), np.arange(GZ), MZ)
    inverse_z = np.block([[cos_b, sin_b], [-sin_b, cos_b]])
    cos_c, sin_c = phases(np.arange(GX), np.arange(MX), MX)
    inverse_x = np.concatenate([cos_c, sin_c], axis=0) / float(MX * MY * MZ)
    forward_hi, forward_lo = hi_lo(forward_z)
    inverse_hi, inverse_lo = hi_lo(inverse_z)
    return dict(
        z_hi=forward_hi,
        z_lo=forward_lo,
        x=stacked_terms(forward_x),
        y=np.stack(forward_y),
        iz_hi=inverse_hi,
        iz_lo=inverse_lo,
        iy=np.stack(inverse_y),
        ix=stacked_terms(inverse_x),
    )


def dot(a, b):
    return jnp.dot(a, b, preferred_element_type=F32)


def split(value):
    top = value.astype(BF16)
    return top, (value - top.astype(F32)).astype(BF16)


def data_terms(value):
    top, rest = split(value)
    return jnp.concatenate([top, rest, top], axis=0)


def deposit_kernel(cell_ref, charge_ref, out_ref):
    cell = cell_ref[...]
    row = ((cell >> 6) & 31) * 8 + (cell >> 13)
    column = ((cell >> 11) & 3) * 64 + (cell & 63)
    index = lax.broadcasted_iota(jnp.int32, (256, cell.shape[1]), 0)
    rows = (index == row).astype(F32).astype(BF16)
    weights = charge_ref[...].astype(F32)
    columns = jnp.where(index == column, weights, 0.0).astype(BF16)
    part = lax.dot_general(
        rows, columns, (((1,), (1,)), ((), ())), preferred_element_type=F32
    )

    @pl.when(pl.program_id(0) == 0)
    def _():
        out_ref[...] = part

    @pl.when(pl.program_id(0) > 0)
    def _():
        out_ref[...] += part


def deposit(cells, charge):
    count = cells.shape[1]
    block = min(DEPOSIT_BLOCK, count)
    return pl.pallas_call(
        deposit_kernel,
        grid=(count // block,),
        in_specs=[
            pl.BlockSpec((1, block), lambda i: (0, i)),
            pl.BlockSpec((1, block), lambda i: (0, i)),
        ],
        out_specs=pl.BlockSpec((256, 256), lambda i: (0, 0)),
        out_shape=jax.ShapeDtypeStruct((256, 256), F32),
        compiler_params=pltpu.CompilerParams(vmem_limit_bytes=32 * 2**20),
        name="deposit",
    )(cells, charge)


def spectral_kernel(
    order_ref,
    density_ref,
    green_ref,
    z_hi_ref,
    z_lo_ref,
    x_ref,
    y_ref,
    iz_hi_ref,
    iz_lo_ref,
    iy_ref,
    ix_ref,
    out_ref,
    after_z,
    after_x,
    total,
    back,
):
    step = pl.program_id(0)
    top, rest = split(density_ref[0])
    after_z[...] = dot(top, z_hi_ref[...]) + (
        dot(rest, z_hi_ref[...]) + dot(top, z_lo_ref[...])
    )
    for pair in range(GY // 2):
        sides = []
        for y in (2 * pair, 2 * pair + 1):
            tiles = [
                after_z[8 * y : 8 * y + 8, (2 * low + part) * MZ : (2 * low + part + 1) * MZ]
                for part in range(2)
                for low in range(4)
            ]
            sides.append(jnp.concatenate(tiles, axis=0))
        out = dot(x_ref[...], data_terms(jnp.concatenate(sides, axis=1)))
        after_x[4 * MZ * pair // 2 : 4 * MZ * pair // 2 + 128, :] = out[:, :MZ]
        after_x[4 * MZ * pair // 2 + 128 : 4 * MZ * pair // 2 + 256, :] = out[:, MZ:]

    @pl.when(step == 0)
    def _():
        total[...] = jnp.zeros_like(total)

    width = green_ref.shape[3]
    for pair in range(MX // 2):
        sides = []
        for kx in (2 * pair, 2 * pair + 1):
            real = after_x[pl.ds(kx, GY, stride=2 * MX), :]
            imag = after_x[pl.ds(MX + kx, GY, stride=2 * MX), :]
            sides.append(jnp.concatenate([real, imag], axis=0))
        out = dot(y_ref[0], data_terms(jnp.concatenate(sides, axis=1)))
        for side in range(2):
            kx = 2 * pair + side
            real = out[:width, side * MZ : (side + 1) * MZ]
            imag = out[width:, side * MZ : (side + 1) * MZ]
            green_real = green_ref[0, 0, kx]
            green_imag = green_ref[0, 1, kx]
            rows = pl.ds(kx * width, width)
            total[rows, :MZ] += green_real * real - green_imag * imag
            total[rows, MZ:] += green_real * imag + green_imag * real

    @pl.when(step == pl.num_programs(0) - 1)
    def _():
        lane = lax.broadcasted_iota(jnp.int32, (GY, 2 * GZ), 1)
        first = lane < GZ
        for group in range(MX // 8):
            top, rest = split(total[group * 8 * width : (group + 1) * 8 * width, :])
            turned = dot(top, iz_hi_ref[...]) + (
                dot(rest, iz_hi_ref[...]) + dot(top, iz_lo_ref[...])
            )
            for pair in range(4):
                sides = [
                    turned[(2 * pair + side) * width : (2 * pair + side + 1) * width, :]
                    for side in range(2)
                ]
                out = dot(iy_ref[0], data_terms(jnp.concatenate(sides, axis=1)))
                for side in range(2):
                    kx = group * 8 + 2 * pair + side
                    by_cos = out[:GY, side * MZ : (side + 1) * MZ]
                    by_sin = pltpu.roll(out[GY:, side * MZ : (side + 1) * MZ], GZ, 1)
                    back[kx * GY : (kx + 1) * GY, :] = by_cos + jnp.where(
                        first, -by_sin, by_sin
                    )
        for pair in range(GY // 2):
            sides = [back[pl.ds(2 * pair + side, MX, stride=GY), :] for side in range(2)]
            out = dot(ix_ref[...], data_terms(jnp.concatenate(sides, axis=1)))
            even = out[:GX, :MZ] - pltpu.roll(out[GX:, :MZ], GZ, 1)
            odd = pltpu.roll(out[:GX, MZ:], GZ, 1) - out[GX:, MZ:]
            out_ref[pair * GX : (pair + 1) * GX, :] = jnp.where(first, even, odd)


def spectral(order, densities, green, tables):
    offsets, _, _, width, _ = green.shape

    def whole(table):
        return pl.BlockSpec(table.shape, lambda i, order: (0,) * table.ndim)

    def by_pencil(table):
        return pl.BlockSpec((1,) + table.shape[1:], lambda i, order: (order[offsets], 0, 0))

    return pl.pallas_call(
        spectral_kernel,
        grid_spec=pltpu.PrefetchScalarGridSpec(
            num_scalar_prefetch=1,
            grid=(offsets,),
            in_specs=[
                pl.BlockSpec((1, 256, 256), lambda i, order: (i, 0, 0)),
                pl.BlockSpec((1, 2, MX, width, MZ), lambda i, order: (order[i], 0, 0, 0, 0)),
                whole(tables["z_hi"]),
                whole(tables["z_lo"]),
                whole(tables["x"]),
                by_pencil(tables["y"]),
                whole(tables["iz_hi"]),
                whole(tables["iz_lo"]),
                by_pencil(tables["iy"]),
                whole(tables["ix"]),
            ],
            out_specs=pl.BlockSpec((512, 128), lambda i, order: (0, 0)),
            scratch_shapes=[
                pltpu.VMEM((256, 1024), F32),
                pltpu.VMEM((GY * 2 * MX, MZ), F32),
                pltpu.VMEM((MX * width, 2 * MZ), F32),
                pltpu.VMEM((MX * GY, 2 * GZ), F32),
            ],
        ),
        out_shape=jax.ShapeDtypeStruct((512, 128), F32),
        compiler_params=pltpu.CompilerParams(vmem_limit_bytes=48 * 2**20),
        name="spectral",
    )(
        order,
        densities,
        green,
        *(tables[name] for name in ("z_hi", "z_lo", "x", "y", "iz_hi", "iz_lo", "iy", "ix")),
    )


def gather_kernel(own_ref, other_ref, cell_ref, out_ref, field):
    @pl.when(pl.program_id(0) == 0)
    def _():
        potential = own_ref[...] + other_ref[...]
        lane = lax.broadcasted_iota(jnp.int32, (512, 128), 1)
        row = lax.broadcasted_iota(jnp.int32, (512, 128), 0)
        x = row % GX
        z = lane % GZ
        zero = jnp.zeros((GX, 128), F32)
        below = jnp.where(x == 0, 0.0, pltpu.roll(potential, 1, 0))
        above = jnp.where(x == GX - 1, 0.0, pltpu.roll(potential, 511, 0))
        field_x = 0.5 * (below - above)
        turned = pltpu.roll(potential, GZ, 1)
        before = jnp.concatenate([zero, turned[: 512 - GX]], axis=0)
        after = jnp.concatenate([turned[GX:], zero], axis=0)
        field_y = 0.5 * (
            jnp.where(lane < GZ, before, turned) - jnp.where(lane < GZ, turned, after)
        )
        left = jnp.where(z == 0, 0.0, pltpu.roll(potential, 1, 1))
        right = jnp.where(z == GZ - 1, 0.0, pltpu.roll(potential, 127, 1))
        field_z = 0.5 * (left - right)
        for part, value in enumerate((field_x, field_y, field_z)):
            field[part * 128 : (part + 1) * 128, :] = jnp.transpose(value).astype(BF16)

    cell = cell_ref[...]
    y = (cell >> 6) & 31
    high = (y >> 1) * GX + (cell >> 11)
    low = (y & 1) * GZ + (cell & 63)
    count = cell.shape[1]
    index = lax.broadcasted_iota(jnp.int32, (512, count), 0)
    chosen = (index == high).astype(F32).astype(BF16)
    picked = dot(field[...], chosen)
    inside = index[:128] == low
    for part in range(3):
        values = jnp.where(inside, picked[part * 128 : (part + 1) * 128], 0.0)
        out_ref[part, :, :] = jnp.sum(values, axis=0, keepdims=True)


def gather(own, other, cells):
    count = cells.shape[1]
    block = min(GATHER_BLOCK, count)
    return pl.pallas_call(
        gather_kernel,
        grid=(count // block,),
        in_specs=[
            pl.BlockSpec((512, 128), lambda i: (0, 0)),
            pl.BlockSpec((512, 128), lambda i: (0, 0)),
            pl.BlockSpec((1, block), lambda i: (0, i)),
        ],
        out_specs=pl.BlockSpec((3, 1, block), lambda i: (0, 0, i)),
        out_shape=jax.ShapeDtypeStruct((3, 1, count), F32),
        scratch_shapes=[pltpu.VMEM((384, 512), BF16)],
        compiler_params=pltpu.CompilerParams(vmem_limit_bytes=32 * 2**20),
        name="gather",
    )(own, other, cells)


def per_device(tables, charge, cell_deposit, cell_gather, green_spectra):
    pencils = lax.axis_size("pencil")
    bunches = lax.axis_size("bunch")
    pencil = lax.axis_index("pencil")
    swap = [(i, (i + 1) % pencils) for i in range(pencils)]
    part = deposit(cell_deposit, charge)
    density = part + lax.ppermute(part, "pencil", swap)
    near = []
    for distance in range(1, SPAN + 1):
        route = []
        for bunch in range(bunches):
            for core, source in ((0, bunch - distance), (1, bunch + distance)):
                if 0 <= source < bunches:
                    route.append((source * pencils + core, bunch * pencils + core))
        near.append(lax.ppermute(density, ("bunch", "pencil"), route))
    near = jnp.stack(near)
    far = lax.ppermute(near, "pencil", swap)
    densities = jnp.concatenate([density[None], near, far], axis=0)
    steps = np.arange(1, SPAN + 1)
    up = np.concatenate([[SPAN], SPAN + steps, SPAN - steps, [0]])
    down = np.concatenate([[SPAN], SPAN - steps, SPAN + steps, [1]])
    order = jnp.where(pencil == 0, jnp.asarray(up, jnp.int32), jnp.asarray(down, jnp.int32))
    own = spectral(order, densities, green_spectra, tables)
    other = lax.ppermute(own, "pencil", swap)
    return gather(own, other, cell_gather)


def solution(mesh):
    in_specs = (
        P(("groups", "bunch"), "pencil"),
        P(("groups", "bunch"), "pencil"),
        P(("groups", "bunch"), "pencil"),
        P(None, None, None, "pencil", None),
    )
    out_specs = P(None, ("groups", "bunch"), "pencil")
    tables = make_tables(mesh.shape["pencil"])
    return jax.shard_map(
        functools.partial(per_device, tables),
        mesh=mesh,
        in_specs=in_specs,
        out_specs=out_specs,
        check_vma=False,
    )
```

profile of v0, /device:TPU:17, one launch (start us, length us, event | category | flops | bytes accessed | tf_op | source)
XLA Modules:
  0.0 65.9 jit_solution(3706557900783299112)
XLA Ops:
  0.0 0.0 copy-start.11
  0.0 0.0 copy-start.12
  0.0 0.0 copy-start.7
  0.0 0.9 %copy-done.7 = s32[1,16384]{1,0:T(1,128)S(1)} copy-done((s32[1,16384]{1,0:T(1,128)S(1)}, s32[1,16384]{1,0:T(1,128)}, u32[]{:S(2)}) %copy-start.7) | copy-done | bytes 65560
  0.9 0.0 copy-start.8
  0.9 0.8 %copy-done.8 = bf16[1,16384]{1,0:T(2,128)(2,1)S(1)} copy-done((bf16[1,16384]{1,0:T(2,128)(2,1)S(1)}, bf16[1,16384]{1,0:T(2,128)(2,1)}, u32[]{:S(2)}) %copy-start.8) | copy-done | bytes 32792
  1.7 4.3 %deposit.1 = f32[256,256]{1,0:T(8,128)S(1)} custom-call(s32[1,16384]{1,0:T(1,128)S(1)} %copy-done.7, bf16[1,16384]{1,0:T(2,128)(2,1)S(1)} %copy-done.8), custom_call_target="tpu_custom_call" | custom-call | tf_op jit(solution)/shard_map/deposit/pallas_call | solution.py:111
  6.1 0.8 %collective-permute-start = (f32[256,256]{1,0:T(8,128)S(1)}, f32[256,256]{1,0:T(8,128)S(1)}, u32[]{:S(2)}, u32[]{:S(2)}) collective-permute-start(f32[256,256]{1,0:T(8,128)S(1)} %deposit.1), channel_id=1, source_target_pairs={{0,1},{1,0},{2,3},{3,2},{4,5},{5,4},{6,7},{7,6},{8,9},{9,8},{10,11... | collective-permute-start | bytes 786440 | tf_op jit(solution)/shard_map/ppermute | solution.py:321
  6.8 1.2 %collective-permute-done = f32[256,256]{1,0:T(8,128)S(1)} collective-permute-done((f32[256,256]{1,0:T(8,128)S(1)}, f32[256,256]{1,0:T(8,128)S(1)}, u32[]{:S(2)}, u32[]{:S(2)}) %collective-permute-start) | collective-permute-done | bytes 262176 | tf_op jit(solution)/shard_map/ppermute | solution.py:321
  8.0 3.0 %collective-permute-start.1 = (f32[256,256]{1,0:T(8,128)S(1)}, f32[256,256]{1,0:T(8,128)S(1)}, u32[]{:S(2)}, u32[]{:S(2)}) collective-permute-start(f32[256,256]{1,0:T(8,128)S(1)} %get-tuple-element.6), channel_id=1, source_target_pairs={{3,1},{0,2},{5,3},{2,4},{7,5},{4,6},{9,7},{6,8},{11,9},{8,10},{13,... | collective-permute-start | bytes 786440 | tf_op jit(solution)/shard_map/ppermute | solution.py:329
  11.0 2.1 %collective-permute-start.2 = (f32[256,256]{1,0:T(8,128)S(1)}, f32[256,256]{1,0:T(8,128)S(1)}, u32[]{:S(2)}, u32[]{:S(2)}) collective-permute-start(f32[256,256]{1,0:T(8,128)S(1)} %get-tuple-element.6), channel_id=1, source_target_pairs={{5,1},{7,3},{0,4},{9,5},{2,6},{11,7},{4,8},{13,9},{6,10},{15,11},{... | collective-permute-start | bytes 786440 | tf_op jit(solution)/shard_map/ppermute | solution.py:329
  13.2 1.9 %collective-permute-start.3 = (f32[256,256]{1,0:T(8,128)S(1)}, f32[256,256]{1,0:T(8,128)S(1)}, u32[]{:S(2)}, u32[]{:S(2)}) collective-permute-start(f32[256,256]{1,0:T(8,128)S(1)} %get-tuple-element.6), channel_id=1, source_target_pairs={{7,1},{9,3},{11,5},{0,6},{13,7},{2,8},{15,9},{4,10},{6,12},{8,14},... | collective-permute-start | bytes 786440 | tf_op jit(solution)/shard_map/ppermute | solution.py:329
  15.1 3.2 %collective-permute-done.1 = f32[256,256]{1,0:T(8,128)S(1)} collective-permute-done((f32[256,256]{1,0:T(8,128)S(1)}, f32[256,256]{1,0:T(8,128)S(1)}, u32[]{:S(2)}, u32[]{:S(2)}) %collective-permute-start.1) | collective-permute-done | bytes 262176 | tf_op jit(solution)/shard_map/ppermute | solution.py:329
  18.3 1.0 %collective-permute-done.2 = f32[256,256]{1,0:T(8,128)S(1)} collective-permute-done((f32[256,256]{1,0:T(8,128)S(1)}, f32[256,256]{1,0:T(8,128)S(1)}, u32[]{:S(2)}, u32[]{:S(2)}) %collective-permute-start.2) | collective-permute-done | bytes 262176 | tf_op jit(solution)/shard_map/ppermute | solution.py:329
  19.2 3.6 %collective-permute-done.3 = f32[256,256]{1,0:T(8,128)S(1)} collective-permute-done((f32[256,256]{1,0:T(8,128)S(1)}, f32[256,256]{1,0:T(8,128)S(1)}, u32[]{:S(2)}, u32[]{:S(2)}) %collective-permute-start.3) | collective-permute-done | bytes 262176 | tf_op jit(solution)/shard_map/ppermute | solution.py:329
  22.8 0.1 pad_maximum_fusion
  22.9 0.0 copy-start
  22.9 0.0 copy-start.1
  22.9 0.0 copy-start.2
  22.9 0.0 copy-start.3
  22.9 0.0 copy-start.4
  22.9 0.0 copy-start.5
  22.9 0.0 copy-start.9
  23.0 0.0 copy-start.10
  23.0 2.8 %collective-permute-start.4 = (f32[3,256,256]{2,1,0:T(8,128)S(1)}, f32[3,256,256]{2,1,0:T(8,128)S(1)}, u32[]{:S(2)}, u32[]{:S(2)}) collective-permute-start(f32[3,256,256]{2,1,0:T(8,128)S(1)} %pad_maximum_fusion), channel_id=1, source_target_pairs={{0,1},{1,0},{2,3},{3,2},{4,5},{5,4},{6,7},{7,6},{8,9},{9,8},{10,11... | collective-permute-start | bytes 2359304 | tf_op jit(solution)/shard_map/ppermute | solution.py:331
  25.7 0.0 copy-done.11
  25.7 0.0 copy-done.12
  25.8 1.8 %collective-permute-done.4 = f32[3,256,256]{2,1,0:T(8,128)S(1)} collective-permute-done((f32[3,256,256]{2,1,0:T(8,128)S(1)}, f32[3,256,256]{2,1,0:T(8,128)S(1)}, u32[]{:S(2)}, u32[]{:S(2)}) %collective-permute-start.4) | collective-permute-done | bytes 786464 | tf_op jit(solution)/shard_map/ppermute | solution.py:331
  27.6 0.1 constant_dynamic-update-slice_fusion.density_ref
  27.7 0.0 copy-done
  27.7 0.0 copy-done.1
  27.7 0.0 copy-done.2
  27.7 0.0 copy-done.3
  27.7 0.0 copy-done.4
  27.7 0.0 copy-done.5
  27.8 0.0 copy-done.9
  27.8 0.0 copy-done.10
  27.8 0.0 copy-start.6
  27.8 24.7 %spectral.1.own_ref = f32[512,128]{1,0:T(8,128)S(1)} custom-call(s32[8]{0:T(128)S(1)} %broadcast_select_fusion.order_ref, f32[7,256,256]{2,1,0:T(8,128)S(1)} %constant_dynamic-update-slice_fusion.density_ref, f32[7,2,64,32,128]{4,3,2,1,0:T(8,128)} %green_ref.1, bf16[256,1024]{1,0:T(8,128)(2,1)S(1)} %copy-done, bf16[256,1024]{1,0:T(8,128)(2,1)S(1)} %copy-done.1, ...), custom_call_target="tpu_custom_call" | custom-call | tf_op jit(solution)/shard_map/spectral/pallas_call | solution.py:222
  52.5 0.5 collective-permute-start.5
  53.0 1.2 %collective-permute-done.5.other_ref = f32[512,128]{1,0:T(8,128)S(1)} collective-permute-done((f32[512,128]{1,0:T(8,128)S(1)}, f32[512,128]{1,0:T(8,128)S(1)}, u32[]{:S(2)}, u32[]{:S(2)}) %collective-permute-start.5) | collective-permute-done | bytes 262176 | tf_op jit(solution)/shard_map/ppermute | solution.py:338
  54.1 0.0 copy-done.6
  54.1 11.7 %gather.1 = f32[3,1,16384]{2,1,0:T(1,128)} custom-call(f32[512,128]{1,0:T(8,128)S(1)} %spectral.1.own_ref, f32[512,128]{1,0:T(8,128)S(1)} %collective-permute-done.5.other_ref, s32[1,16384]{1,0:T(1,128)S(1)} %copy-done.6), custom_call_target="tpu_custom_call" | custom-call | tf_op jit(solution)/shard_map/gather/pallas_call | solution.py:299
  (5 shorter events, 0.1 us)
Async XLA Ops:
  0.0 25.7 %copy-start.11 = (s32[8]{0:T(128)S(1)}, s32[8]{0:T(128)}, u32[]{:S(2)}) copy-start(s32[8]{0:T(128)} %constant.26.clone) | copy-start | bytes 100
  0.0 25.7 %copy-start.12 = (s32[8]{0:T(128)S(1)}, s32[8]{0:T(128)}, u32[]{:S(2)}) copy-start(s32[8]{0:T(128)} %constant.27.clone) | copy-start | bytes 100
  0.0 0.9 %copy-start.7 = (s32[1,16384]{1,0:T(1,128)S(1)}, s32[1,16384]{1,0:T(1,128)}, u32[]{:S(2)}) copy-start(s32[1,16384]{1,0:T(1,128)} %cell_ref.2) | copy-start | bytes 196612
  0.9 0.8 %copy-start.8 = (bf16[1,16384]{1,0:T(2,128)(2,1)S(1)}, bf16[1,16384]{1,0:T(2,128)(2,1)}, u32[]{:S(2)}) copy-start(bf16[1,16384]{1,0:T(2,128)(2,1)} %charge_ref.1) | copy-start | bytes 98308
  6.1 1.9 %collective-permute-start = (f32[256,256]{1,0:T(8,128)S(1)}, f32[256,256]{1,0:T(8,128)S(1)}, u32[]{:S(2)}, u32[]{:S(2)}) collective-permute-start(f32[256,256]{1,0:T(8,128)S(1)} %deposit.1), channel_id=1, source_target_pairs={{0,1},{1,0},{2,3},{3,2},{4,5},{5,4},{6,7},{7,6},{8,9},{9,8},{10,11... | collective-permute-start | bytes 786440 | tf_op jit(solution)/shard_map/ppermute | solution.py:321
  8.0 10.2 %collective-permute-start.1 = (f32[256,256]{1,0:T(8,128)S(1)}, f32[256,256]{1,0:T(8,128)S(1)}, u32[]{:S(2)}, u32[]{:S(2)}) collective-permute-start(f32[256,256]{1,0:T(8,128)S(1)} %get-tuple-element.6), channel_id=1, source_target_pairs={{3,1},{0,2},{5,3},{2,4},{7,5},{4,6},{9,7},{6,8},{11,9},{8,10},{13,... | collective-permute-start | bytes 786440 | tf_op jit(solution)/shard_map/ppermute | solution.py:329
  11.0 8.2 %collective-permute-start.2 = (f32[256,256]{1,0:T(8,128)S(1)}, f32[256,256]{1,0:T(8,128)S(1)}, u32[]{:S(2)}, u32[]{:S(2)}) collective-permute-start(f32[256,256]{1,0:T(8,128)S(1)} %get-tuple-element.6), channel_id=1, source_target_pairs={{5,1},{7,3},{0,4},{9,5},{2,6},{11,7},{4,8},{13,9},{6,10},{15,11},{... | collective-permute-start | bytes 786440 | tf_op jit(solution)/shard_map/ppermute | solution.py:329
  13.2 9.7 %collective-permute-start.3 = (f32[256,256]{1,0:T(8,128)S(1)}, f32[256,256]{1,0:T(8,128)S(1)}, u32[]{:S(2)}, u32[]{:S(2)}) collective-permute-start(f32[256,256]{1,0:T(8,128)S(1)} %get-tuple-element.6), channel_id=1, source_target_pairs={{7,1},{9,3},{11,5},{0,6},{13,7},{2,8},{15,9},{4,10},{6,12},{8,14},... | collective-permute-start | bytes 786440 | tf_op jit(solution)/shard_map/ppermute | solution.py:329
  22.9 4.8 %copy-start = (bf16[256,1024]{1,0:T(8,128)(2,1)S(1)}, bf16[256,1024]{1,0:T(8,128)(2,1)}, u32[]{:S(2)}) copy-start(bf16[256,1024]{1,0:T(8,128)(2,1)} %constant.28.clone.z_hi_ref) | copy-start | bytes 1572868
  22.9 4.8 %copy-start.1 = (bf16[256,1024]{1,0:T(8,128)(2,1)S(1)}, bf16[256,1024]{1,0:T(8,128)(2,1)}, u32[]{:S(2)}) copy-start(bf16[256,1024]{1,0:T(8,128)(2,1)} %constant.29.clone.z_lo_ref) | copy-start | bytes 1572868
  22.9 4.8 %copy-start.2 = (bf16[128,192]{1,0:T(8,128)(2,1)S(1)}, bf16[128,192]{1,0:T(8,128)(2,1)}, u32[]{:S(2)}) copy-start(bf16[128,192]{1,0:T(8,128)(2,1)} %constant.30.clone.x_ref) | copy-start | bytes 147460
  22.9 4.8 %copy-start.3 = (bf16[2,64,192]{2,1,0:T(8,128)(2,1)S(1)}, bf16[2,64,192]{2,1,0:T(8,128)(2,1)}, u32[]{:S(2)}) copy-start(bf16[2,64,192]{2,1,0:T(8,128)(2,1)} %constant.31.clone.y_ref) | copy-start | bytes 147460
  22.9 4.8 %copy-start.4 = (bf16[256,128]{1,0:T(8,128)(2,1)S(1)}, bf16[256,128]{1,0:T(8,128)(2,1)}, u32[]{:S(2)}) copy-start(bf16[256,128]{1,0:T(8,128)(2,1)} %constant.32.clone.iz_hi_ref) | copy-start | bytes 196612
  22.9 4.8 %copy-start.5 = (bf16[256,128]{1,0:T(8,128)(2,1)S(1)}, bf16[256,128]{1,0:T(8,128)(2,1)}, u32[]{:S(2)}) copy-start(bf16[256,128]{1,0:T(8,128)(2,1)} %constant.33.clone.iz_lo_ref) | copy-start | bytes 196612
  22.9 4.8 %copy-start.9 = (bf16[2,64,96]{2,1,0:T(8,128)(2,1)S(1)}, bf16[2,64,96]{2,1,0:T(8,128)(2,1)}, u32[]{:S(2)}) copy-start(bf16[2,64,96]{2,1,0:T(8,128)(2,1)} %constant.34.clone.iy_ref) | copy-start | bytes 73732
  23.0 4.8 %copy-start.10 = (bf16[64,192]{1,0:T(8,128)(2,1)S(1)}, bf16[64,192]{1,0:T(8,128)(2,1)}, u32[]{:S(2)}) copy-start(bf16[64,192]{1,0:T(8,128)(2,1)} %constant.35.clone.ix_ref) | copy-start | bytes 73732
  23.0 4.7 %collective-permute-start.4 = (f32[3,256,256]{2,1,0:T(8,128)S(1)}, f32[3,256,256]{2,1,0:T(8,128)S(1)}, u32[]{:S(2)}, u32[]{:S(2)}) collective-permute-start(f32[3,256,256]{2,1,0:T(8,128)S(1)} %pad_maximum_fusion), channel_id=1, source_target_pairs={{0,1},{1,0},{2,3},{3,2},{4,5},{5,4},{6,7},{7,6},{8,9},{9,8},{10,11... | collective-permute-start | bytes 2359304 | tf_op jit(solution)/shard_map/ppermute | solution.py:331
  27.8 26.4 %copy-start.6 = (s32[1,16384]{1,0:T(1,128)S(1)}, s32[1,16384]{1,0:T(1,128)}, u32[]{:S(2)}) copy-start(s32[1,16384]{1,0:T(1,128)} %cell_ref.3) | copy-start | bytes 196612
  52.5 1.6 %collective-permute-start.5 = (f32[512,128]{1,0:T(8,128)S(1)}, f32[512,128]{1,0:T(8,128)S(1)}, u32[]{:S(2)}, u32[]{:S(2)}) collective-permute-start(f32[512,128]{1,0:T(8,128)S(1)} %spectral.1.own_ref), channel_id=1, source_target_pairs={{0,1},{1,0},{2,3},{3,2},{4,5},{5,4},{6,7},{7,6},{8,9},{9,8},{10,11... | collective-permute-start | bytes 786440 | tf_op jit(solution)/shard_map/ppermute | solution.py:338
where the time goes:
time: 67.2 us; the launch traced here: 65.9 us
  Pallas kernels  40.8 us (61%)
  waiting for transfers between devices  11.9 us (18%)
  starting transfers between devices  11 us (16%)
  local copies, waits for them, and re-layouts  1.88 us (3%)
    pallas_call x1, Pallas kernels, spectral(): pl.pallas_call(spectral_kernel, grid_spec=pltpu.PrefetchScalarGridSpec(nu...  24.7 us
    pallas_call x1, Pallas kernels, gather(): pl.pallas_call(gather_kernel, grid=(count // block,), in_specs=[pl.BlockS...  11.7 us
    ppermute x3, waiting for transfers between devices, per_device(): near.append(lax.ppermute(density, ('bunch', 'pencil'), route))  7.72 us
    ppermute x3, starting transfers between devices, per_device(): near.append(lax.ppermute(density, ('bunch', 'pencil'), route))  7.03 us
    pallas_call x1, Pallas kernels, deposit(): pl.pallas_call(deposit_kernel, grid=(count // block,), in_specs=[pl.Block...  4.34 us
    ppermute x1, starting transfers between devices, per_device(): far = lax.ppermute(near, 'pencil', swap)  2.76 us
    unnamed x29, local copies, waits for them, and re-layouts  1.83 us
    ppermute x1, waiting for transfers between devices, per_device(): far = lax.ppermute(near, 'pencil', swap)  1.82 us
  transfers between devices with their start and end apart: 6, of which 6 were waited for; matrix products, arithmetic and copies ran while one was open for 0% of the time, Pallas kernels for 0%

commit v1 on v0

v1 whole, which is shorter than its diff:
```python
import functools

import jax
import jax.numpy as jnp
import numpy as np
from jax import lax
from jax.experimental import pallas as pl
from jax.experimental.pallas import tpu as pltpu
from jax.sharding import PartitionSpec as P

GX = 32
GY = 32
GZ = 64
SPAN = 3
MX = 64
MY = 64
MZ = 128
BF16 = jnp.bfloat16
F32 = jnp.float32
GATHER_CHUNK = 512
PITCH_X = 2 * MX + 1
PITCH_Y = GY + 1


def hi_lo(table):
    top = table.astype(np.float32).astype(BF16)
    rest = (table - top.astype(np.float64)).astype(np.float32).astype(BF16)
    return top, rest


def stacked_terms(table):
    top, rest = hi_lo(table)
    return np.concatenate([top, top, rest], axis=-1)


def phases(rows, columns, period):
    angles = 2.0 * np.pi / period * ((rows[:, None] * columns[None, :]) % period)
    return np.cos(angles), np.sin(angles)


def make_tables(pencils):
    width = MY // pencils
    cos_z, sin_z = phases(np.arange(GZ), np.arange(MZ), MZ)
    forward_z = np.concatenate([cos_z, -sin_z], axis=1)
    grid_x = (np.arange(8)[None, :] * 4 + np.arange(4)[:, None]).reshape(-1)
    cos_x, sin_x = phases(np.arange(MX), grid_x, MX)
    forward_x = np.block([[cos_x, sin_x], [-sin_x, cos_x]])
    forward_y = []
    inverse_y = []
    for pencil in range(pencils):
        own = np.arange(pencil * width, (pencil + 1) * width)
        cos_y, sin_y = phases(own, np.arange(GY), MY)
        forward_y.append(stacked_terms(np.block([[cos_y, sin_y], [-sin_y, cos_y]])))
        inverse_y.append(stacked_terms(np.concatenate([cos_y.T, sin_y.T], axis=0)))
    cos_b, sin_b = phases(np.arange(MZ), np.arange(GZ), MZ)
    inverse_z = np.block([[cos_b, sin_b], [-sin_b, cos_b]])
    cos_c, sin_c = phases(np.arange(GX), np.arange(MX), MX)
    inverse_x = np.concatenate([cos_c, sin_c], axis=0) / float(MX * MY * MZ)
    inverse_hi, inverse_lo = hi_lo(inverse_z)
    return dict(
        z=stacked_terms(forward_z.T).T,
        x=stacked_terms(forward_x),
        y=np.stack(forward_y),
        iz_hi=inverse_hi,
        iz_lo=inverse_lo,
        iy=np.stack(inverse_y),
        ix=stacked_terms(inverse_x),
    )


def dot(a, b):
    return jnp.dot(a, b, preferred_element_type=F32)


def split(value):
    top = value.astype(BF16)
    return top, (value - top.astype(F32)).astype(BF16)


def data_terms(value):
    top, rest = split(value)
    return jnp.concatenate([top, rest, top], axis=0)


def one_hot(index, rows, value):
    place = lax.broadcasted_iota(jnp.int16, (rows, index.shape[1]), 0)
    return jnp.where(place == index.astype(jnp.int16), value, jnp.zeros((), BF16))


def deposit_kernel(cell_ref, charge_ref, out_ref):
    cell = cell_ref[...]
    row = ((cell >> 6) & 31) * 8 + (cell >> 13)
    column = ((cell >> 11) & 3) * 64 + (cell & 63)
    out_ref[...] = lax.dot_general(
        one_hot(row, 256, jnp.ones((), BF16)),
        one_hot(column, 256, charge_ref[...]),
        (((1,), (1,)), ((), ())),
        preferred_element_type=F32,
    )


def deposit(cells, charge):
    return pl.pallas_call(
        deposit_kernel,
        out_shape=jax.ShapeDtypeStruct((256, 256), F32),
        compiler_params=pltpu.CompilerParams(vmem_limit_bytes=48 * 2**20),
        name="deposit",
    )(cells, charge)


def spectral_kernel(
    order_ref,
    density_ref,
    green_ref,
    z_ref,
    x_ref,
    y_ref,
    iz_hi_ref,
    iz_lo_ref,
    iy_ref,
    ix_ref,
    out_ref,
    after_z,
    after_x,
    total,
    back,
):
    step = pl.program_id(0)
    top, rest = split(density_ref[0])
    for low in range(4):
        lanes = slice(low * GZ, (low + 1) * GZ)
        terms = jnp.concatenate([top[:, lanes], rest[:, lanes], top[:, lanes]], axis=1)
        after_z[:, 2 * MZ * low : 2 * MZ * (low + 1)] = dot(terms, z_ref[...])
    for pair in range(GY // 2):
        sides = []
        for y in (2 * pair, 2 * pair + 1):
            tiles = [
                after_z[8 * y : 8 * y + 8, (2 * low + part) * MZ : (2 * low + part + 1) * MZ]
                for part in range(2)
                for low in range(4)
            ]
            sides.append(jnp.concatenate(tiles, axis=0))
        out = dot(x_ref[...], data_terms(jnp.concatenate(sides, axis=1)))
        for side in range(2):
            rows = pl.ds((2 * pair + side) * PITCH_X, 2 * MX)
            after_x[rows, :] = out[:, side * MZ : (side + 1) * MZ]

    @pl.when(step == 0)
    def _():
        total[...] = jnp.zeros_like(total)

    width = green_ref.shape[3]
    for pair in range(MX // 2):
        sides = []
        for kx in (2 * pair, 2 * pair + 1):
            real = after_x[pl.ds(kx, GY, stride=PITCH_X), :]
            imag = after_x[pl.ds(MX + kx, GY, stride=PITCH_X), :]
            sides.append(jnp.concatenate([real, imag], axis=0))
        out = dot(y_ref[0], data_terms(jnp.concatenate(sides, axis=1)))
        for side in range(2):
            kx = 2 * pair + side
            real = out[:width, side * MZ : (side + 1) * MZ]
            imag = out[width:, side * MZ : (side + 1) * MZ]
            green_real = green_ref[0, 0, kx]
            green_imag = green_ref[0, 1, kx]
            rows = pl.ds(kx * width, width)
            total[rows, :MZ] += green_real * real - green_imag * imag
            total[rows, MZ:] += green_real * imag + green_imag * real

    @pl.when(step == pl.num_programs(0) - 1)
    def _():
        lane = lax.broadcasted_iota(jnp.int32, (GY, 2 * GZ), 1)
        first = lane < GZ
        for group in range(MX // 8):
            top, rest = split(total[group * 8 * width : (group + 1) * 8 * width, :])
            turned = dot(top, iz_hi_ref[...]) + (
                dot(rest, iz_hi_ref[...]) + dot(top, iz_lo_ref[...])
            )
            for pair in range(4):
                sides = [
                    turned[(2 * pair + side) * width : (2 * pair + side + 1) * width, :]
                    for side in range(2)
                ]
                out = dot(iy_ref[0], data_terms(jnp.concatenate(sides, axis=1)))
                for side in range(2):
                    kx = group * 8 + 2 * pair + side
                    by_cos = out[:GY, side * MZ : (side + 1) * MZ]
                    by_sin = pltpu.roll(out[GY:, side * MZ : (side + 1) * MZ], GZ, 1)
                    back[pl.ds(kx * PITCH_Y, GY), :] = by_cos + jnp.where(
                        first, -by_sin, by_sin
                    )
        for pair in range(GY // 2):
            sides = [back[pl.ds(2 * pair + side, MX, stride=PITCH_Y), :] for side in range(2)]
            out = dot(ix_ref[...], data_terms(jnp.concatenate(sides, axis=1)))
            even = out[:GX, :MZ] - pltpu.roll(out[GX:, :MZ], GZ, 1)
            odd = pltpu.roll(out[:GX, MZ:], GZ, 1) - out[GX:, MZ:]
            out_ref[pair * GX : (pair + 1) * GX, :] = jnp.where(first, even, odd)


def spectral(order, densities, green, tables):
    offsets, _, _, width, _ = green.shape

    def whole(table):
        return pl.BlockSpec(table.shape, lambda i, order: (0,) * table.ndim)

    def by_pencil(table):
        return pl.BlockSpec((1,) + table.shape[1:], lambda i, order: (order[offsets], 0, 0))

    return pl.pallas_call(
        spectral_kernel,
        grid_spec=pltpu.PrefetchScalarGridSpec(
            num_scalar_prefetch=1,
            grid=(offsets,),
            in_specs=[
                pl.BlockSpec((1, 256, 256), lambda i, order: (i, 0, 0)),
                pl.BlockSpec((1, 2, MX, width, MZ), lambda i, order: (order[i], 0, 0, 0, 0)),
                whole(tables["z"]),
                whole(tables["x"]),
                by_pencil(tables["y"]),
                whole(tables["iz_hi"]),
                whole(tables["iz_lo"]),
                by_pencil(tables["iy"]),
                whole(tables["ix"]),
            ],
            out_specs=pl.BlockSpec((512, 128), lambda i, order: (0, 0)),
            scratch_shapes=[
                pltpu.VMEM((256, 1024), F32),
                pltpu.VMEM((GY * PITCH_X, MZ), F32),
                pltpu.VMEM((MX * width, 2 * MZ), F32),
                pltpu.VMEM((MX * PITCH_Y, 2 * GZ), F32),
            ],
        ),
        out_shape=jax.ShapeDtypeStruct((512, 128), F32),
        compiler_params=pltpu.CompilerParams(vmem_limit_bytes=48 * 2**20),
        name="spectral",
    )(
        order,
        densities,
        green,
        *(tables[name] for name in ("z", "x", "y", "iz_hi", "iz_lo", "iy", "ix")),
    )


def gather_kernel(own_ref, other_ref, cell_ref, out_ref, field):
    potential = own_ref[...] + other_ref[...]
    lane = lax.broadcasted_iota(jnp.int32, (512, 128), 1)
    row = lax.broadcasted_iota(jnp.int32, (512, 128), 0)
    x = row % GX
    z = lane % GZ
    zero = jnp.zeros((GX, 128), F32)
    below = jnp.where(x == 0, 0.0, pltpu.roll(potential, 1, 0))
    above = jnp.where(x == GX - 1, 0.0, pltpu.roll(potential, 511, 0))
    field_x = 0.5 * (below - above)
    turned = pltpu.roll(potential, GZ, 1)
    before = jnp.concatenate([zero, turned[: 512 - GX]], axis=0)
    after = jnp.concatenate([turned[GX:], zero], axis=0)
    field_y = 0.5 * (
        jnp.where(lane < GZ, before, turned) - jnp.where(lane < GZ, turned, after)
    )
    left = jnp.where(z == 0, 0.0, pltpu.roll(potential, 1, 1))
    right = jnp.where(z == GZ - 1, 0.0, pltpu.roll(potential, 127, 1))
    field_z = 0.5 * (left - right)
    for part, value in enumerate((field_x, field_y, field_z)):
        field[part * 128 : (part + 1) * 128, :] = jnp.transpose(value).astype(BF16)

    count = cell_ref.shape[1]
    chunk = min(GATHER_CHUNK, count)
    for at in range(0, count, chunk):
        cell = cell_ref[:, at : at + chunk]
        y = (cell >> 6) & 31
        high = (y >> 1) * GX + (cell >> 11)
        low = (y & 1) * GZ + (cell & 63)
        picked = dot(field[...], one_hot(high, 512, jnp.ones((), BF16)))
        inside = lax.broadcasted_iota(jnp.int32, (128, chunk), 0) == low
        for part in range(3):
            values = jnp.where(inside, picked[part * 128 : (part + 1) * 128], 0.0)
            out_ref[part, :, at : at + chunk] = jnp.sum(values, axis=0, keepdims=True)


def gather(own, other, cells):
    return pl.pallas_call(
        gather_kernel,
        out_shape=jax.ShapeDtypeStruct((3, 1, cells.shape[1]), F32),
        scratch_shapes=[pltpu.VMEM((384, 512), BF16)],
        compiler_params=pltpu.CompilerParams(vmem_limit_bytes=48 * 2**20),
        name="gather",
    )(own, other, cells)


def per_device(tables, charge, cell_deposit, cell_gather, green_spectra):
    pencils = lax.axis_size("pencil")
    bunches = lax.axis_size("bunch")
    pencil = lax.axis_index("pencil")
    swap = [(i, (i + 1) % pencils) for i in range(pencils)]
    part = deposit(cell_deposit, charge)
    density = part + lax.ppermute(part, "pencil", swap)
    near = []
    for distance in range(SPAN, 0, -1):
        route = []
        for bunch in range(distance, bunches):
            ends = (bunch * pencils, (bunch - distance) * pencils + 1)
            route.extend([ends, ends[::-1]])
        near.append(lax.ppermute(density, ("bunch", "pencil"), route))
    near = jnp.stack(near)
    far = lax.ppermute(near, "pencil", swap)
    densities = jnp.concatenate([density[None], near, far], axis=0)
    steps = np.arange(SPAN, 0, -1)
    up = np.concatenate([[SPAN], SPAN + steps, SPAN - steps, [0]])
    down = np.concatenate([[SPAN], SPAN - steps, SPAN + steps, [1]])
    order = jnp.where(pencil == 0, jnp.asarray(up, jnp.int32), jnp.asarray(down, jnp.int32))
    own = spectral(order, densities, green_spectra, tables)
    other = lax.ppermute(own, "pencil", swap)
    return gather(own, other, cell_gather)


def solution(mesh):
    in_specs = (
        P(("groups", "bunch"), "pencil"),
        P(("groups", "bunch"), "pencil"),
        P(("groups", "bunch"), "pencil"),
        P(None, None, None, "pencil", None),
    )
    out_specs = P(None, ("groups", "bunch"), "pencil")
    tables = make_tables(mesh.shape["pencil"])
    return jax.shard_map(
        functools.partial(per_device, tables),
        mesh=mesh,
        in_specs=in_specs,
        out_specs=out_specs,
        check_vma=False,
    )
```

time: 67.2 us -> 53.4 us (0.79); the launches traced: 65.9 us -> 53.1 us
  Pallas kernels: 40.8 us -> 27.3 us
  starting transfers between devices: 11 us -> 13.4 us
  waiting for transfers between devices: 11.9 us -> 10.2 us
    pallas_call x1, Pallas kernels: 24.7 us -> 16.3 us  [spectral(): pl.pallas_call(spectral_kernel, grid_spec=pltpu.PrefetchScalarGridSpec(nu...]
    pallas_call x2, Pallas kernels: 16.1 us -> 10.9 us  [the longest x1 8.57 us: gather(): pl.pallas_call(gather_kernel, out_shape=jax.ShapeDtypeStruct((3, 1, cells...]
    ppermute x3, starting transfers between devices: 7.03 us -> 9.93 us  [per_device(): near.append(lax.ppermute(density, ('bunch', 'pencil'), route))]
    ppermute x3, waiting for transfers between devices: 7.72 us -> 6.1 us  [per_device(): near.append(lax.ppermute(density, ('bunch', 'pencil'), route))]
    unnamed x29 -> x27, local copies, waits for them, and re-layouts: 1.83 us -> 1.82 us
where the time goes in v1:
time: 53.4 us; the launch traced here: 53.1 us
  Pallas kernels  27.3 us (51%)
  starting transfers between devices  13.4 us (25%)
  waiting for transfers between devices  10.2 us (19%)
  local copies, waits for them, and re-layouts  1.87 us (4%)
    pallas_call x1, Pallas kernels, spectral(): pl.pallas_call(spectral_kernel, grid_spec=pltpu.PrefetchScalarGridSpec(nu...  16.3 us
    ppermute x3, starting transfers between devices, per_device(): near.append(lax.ppermute(density, ('bunch', 'pencil'), route))  9.93 us
    pallas_call x1, Pallas kernels, gather(): pl.pallas_call(gather_kernel, out_shape=jax.ShapeDtypeStruct((3, 1, cells...  8.57 us
    ppermute x3, waiting for transfers between devices, per_device(): near.append(lax.ppermute(density, ('bunch', 'pencil'), route))  6.1 us
    pallas_call x1, Pallas kernels, deposit(): pl.pallas_call(deposit_kernel, out_shape=jax.ShapeDtypeStruct((256, 256),...  2.37 us
    ppermute x1, starting transfers between devices, per_device(): far = lax.ppermute(near, 'pencil', swap)  2.3 us
    unnamed x27, local copies, waits for them, and re-layouts  1.82 us
    ppermute x1, waiting for transfers between devices, per_device(): far = lax.ppermute(near, 'pencil', swap)  1.82 us
  transfers between devices with their start and end apart: 6, of which 6 were waited for; matrix products, arithmetic and copies ran while one was open for 0% of the time, Pallas kernels for 0%

profile of v1, /device:TPU:17, one launch (start us, length us, event | category | flops | bytes accessed | tf_op | source)
XLA Modules:
  0.0 53.1 jit_solution(5220117056239744211)
XLA Ops:
  0.0 0.0 copy-start.10
  0.0 0.0 copy-start.11
  0.0 0.0 copy-start.6
  0.0 0.9 %copy-done.6 = s32[1,16384]{1,0:T(1,128)S(1)} copy-done((s32[1,16384]{1,0:T(1,128)S(1)}, s32[1,16384]{1,0:T(1,128)}, u32[]{:S(2)}) %copy-start.6) | copy-done | bytes 65560
  0.9 0.0 copy-start.7
  0.9 0.8 %copy-done.7 = bf16[1,16384]{1,0:T(2,128)(2,1)S(1)} copy-done((bf16[1,16384]{1,0:T(2,128)(2,1)S(1)}, bf16[1,16384]{1,0:T(2,128)(2,1)}, u32[]{:S(2)}) %copy-start.7) | copy-done | bytes 32792
  1.7 2.4 %deposit.1 = f32[256,256]{1,0:T(8,128)S(1)} custom-call(s32[1,16384]{1,0:T(1,128)S(1)} %copy-done.6, bf16[1,16384]{1,0:T(2,128)(2,1)S(1)} %copy-done.7), custom_call_target="tpu_custom_call" | custom-call | tf_op jit(solution)/shard_map/deposit/pallas_call | solution.py:103
  4.1 0.7 %collective-permute-start = (f32[256,256]{1,0:T(8,128)S(1)}, f32[256,256]{1,0:T(8,128)S(1)}, u32[]{:S(2)}, u32[]{:S(2)}) collective-permute-start(f32[256,256]{1,0:T(8,128)S(1)} %deposit.1), channel_id=1, source_target_pairs={{0,1},{1,0},{2,3},{3,2},{4,5},{5,4},{6,7},{7,6},{8,9},{9,8},{10,11... | collective-permute-start | bytes 786440 | tf_op jit(solution)/shard_map/ppermute | solution.py:296
  4.8 1.2 %collective-permute-done = f32[256,256]{1,0:T(8,128)S(1)} collective-permute-done((f32[256,256]{1,0:T(8,128)S(1)}, f32[256,256]{1,0:T(8,128)S(1)}, u32[]{:S(2)}, u32[]{:S(2)}) %collective-permute-start) | collective-permute-done | bytes 262176 | tf_op jit(solution)/shard_map/ppermute | solution.py:296
  6.0 4.4 %collective-permute-start.1 = (f32[256,256]{1,0:T(8,128)S(1)}, f32[256,256]{1,0:T(8,128)S(1)}, u32[]{:S(2)}, u32[]{:S(2)}) collective-permute-start(f32[256,256]{1,0:T(8,128)S(1)} %get-tuple-element.6), channel_id=1, source_target_pairs={{6,1},{1,6},{8,3},{3,8},{10,5},{5,10},{12,7},{7,12},{14,9},{9,14},... | collective-permute-start | bytes 786440 | tf_op jit(solution)/shard_map/ppermute | solution.py:303
  10.5 2.0 %collective-permute-start.2 = (f32[256,256]{1,0:T(8,128)S(1)}, f32[256,256]{1,0:T(8,128)S(1)}, u32[]{:S(2)}, u32[]{:S(2)}) collective-permute-start(f32[256,256]{1,0:T(8,128)S(1)} %get-tuple-element.6), channel_id=1, source_target_pairs={{4,1},{1,4},{6,3},{3,6},{8,5},{5,8},{10,7},{7,10},{12,9},{9,12},{1... | collective-permute-start | bytes 786440 | tf_op jit(solution)/shard_map/ppermute | solution.py:303
  12.4 3.5 %collective-permute-start.3 = (f32[256,256]{1,0:T(8,128)S(1)}, f32[256,256]{1,0:T(8,128)S(1)}, u32[]{:S(2)}, u32[]{:S(2)}) collective-permute-start(f32[256,256]{1,0:T(8,128)S(1)} %get-tuple-element.6), channel_id=1, source_target_pairs={{2,1},{1,2},{4,3},{3,4},{6,5},{5,6},{8,7},{7,8},{10,9},{9,10},{12,... | collective-permute-start | bytes 786440 | tf_op jit(solution)/shard_map/ppermute | solution.py:303
  16.0 1.2 %collective-permute-done.1 = f32[256,256]{1,0:T(8,128)S(1)} collective-permute-done((f32[256,256]{1,0:T(8,128)S(1)}, f32[256,256]{1,0:T(8,128)S(1)}, u32[]{:S(2)}, u32[]{:S(2)}) %collective-permute-start.1) | collective-permute-done | bytes 262176 | tf_op jit(solution)/shard_map/ppermute | solution.py:303
  17.2 1.1 %collective-permute-done.2 = f32[256,256]{1,0:T(8,128)S(1)} collective-permute-done((f32[256,256]{1,0:T(8,128)S(1)}, f32[256,256]{1,0:T(8,128)S(1)}, u32[]{:S(2)}, u32[]{:S(2)}) %collective-permute-start.2) | collective-permute-done | bytes 262176 | tf_op jit(solution)/shard_map/ppermute | solution.py:303
  18.2 3.9 %collective-permute-done.3 = f32[256,256]{1,0:T(8,128)S(1)} collective-permute-done((f32[256,256]{1,0:T(8,128)S(1)}, f32[256,256]{1,0:T(8,128)S(1)}, u32[]{:S(2)}, u32[]{:S(2)}) %collective-permute-start.3) | collective-permute-done | bytes 262176 | tf_op jit(solution)/shard_map/ppermute | solution.py:303
  22.1 0.1 pad_maximum_fusion
  22.1 0.0 copy-start
  22.1 0.0 copy-start.1
  22.2 0.0 copy-start.2
  22.2 0.0 copy-start.3
  22.2 0.0 copy-start.4
  22.2 0.0 copy-start.8
  22.2 0.0 copy-start.9
  22.2 2.3 %collective-permute-start.4 = (f32[3,256,256]{2,1,0:T(8,128)S(1)}, f32[3,256,256]{2,1,0:T(8,128)S(1)}, u32[]{:S(2)}, u32[]{:S(2)}) collective-permute-start(f32[3,256,256]{2,1,0:T(8,128)S(1)} %pad_maximum_fusion), channel_id=1, source_target_pairs={{0,1},{1,0},{2,3},{3,2},{4,5},{5,4},{6,7},{7,6},{8,9},{9,8},{10,11... | collective-permute-start | bytes 2359304 | tf_op jit(solution)/shard_map/ppermute | solution.py:305
  24.5 0.0 copy-done.10
  24.5 0.0 copy-done.11
  24.6 1.8 %collective-permute-done.4 = f32[3,256,256]{2,1,0:T(8,128)S(1)} collective-permute-done((f32[3,256,256]{2,1,0:T(8,128)S(1)}, f32[3,256,256]{2,1,0:T(8,128)S(1)}, u32[]{:S(2)}, u32[]{:S(2)}) %collective-permute-start.4) | collective-permute-done | bytes 786464 | tf_op jit(solution)/shard_map/ppermute | solution.py:305
  26.4 0.1 constant_dynamic-update-slice_fusion.density_ref
  26.5 0.0 copy-done
  26.5 0.0 copy-done.1
  26.5 0.0 copy-done.2
  26.5 0.0 copy-done.3
  26.5 0.0 copy-done.4
  26.6 0.0 copy-done.8
  26.6 0.0 copy-done.9
  26.6 0.0 copy-start.5
  26.6 16.3 %spectral.1.own_ref = f32[512,128]{1,0:T(8,128)S(1)} custom-call(s32[8]{0:T(128)S(1)} %broadcast_select_fusion.order_ref, f32[7,256,256]{2,1,0:T(8,128)S(1)} %constant_dynamic-update-slice_fusion.density_ref, f32[7,2,64,32,128]{4,3,2,1,0:T(8,128)} %green_ref.1, bf16[192,256]{1,0:T(8,128)(2,1)S(1)} %copy-done, bf16[128,192]{1,0:T(8,128)(2,1)S(1)} %copy-done.1, ...), custom_call_target="tpu_custom_call" | custom-call | tf_op jit(solution)/shard_map/spectral/pallas_call | solution.py:209
  42.9 0.4 collective-permute-start.5
  43.4 1.2 %collective-permute-done.5.other_ref = f32[512,128]{1,0:T(8,128)S(1)} collective-permute-done((f32[512,128]{1,0:T(8,128)S(1)}, f32[512,128]{1,0:T(8,128)S(1)}, u32[]{:S(2)}, u32[]{:S(2)}) %collective-permute-start.5) | collective-permute-done | bytes 262176 | tf_op jit(solution)/shard_map/ppermute | solution.py:312
  44.5 0.0 copy-done.5
  44.5 8.6 %gather.1 = f32[3,1,16384]{2,1,0:T(1,128)} custom-call(f32[512,128]{1,0:T(8,128)S(1)} %spectral.1.own_ref, f32[512,128]{1,0:T(8,128)S(1)} %collective-permute-done.5.other_ref, s32[1,16384]{1,0:T(1,128)S(1)} %copy-done.5), custom_call_target="tpu_custom_call" | custom-call | tf_op jit(solution)/shard_map/gather/pallas_call | solution.py:281
  (5 shorter events, 0.1 us)
Async XLA Ops:
  0.0 24.5 %copy-start.10 = (s32[8]{0:T(128)S(1)}, s32[8]{0:T(128)}, u32[]{:S(2)}) copy-start(s32[8]{0:T(128)} %constant.24.clone) | copy-start | bytes 100
  0.0 24.5 %copy-start.11 = (s32[8]{0:T(128)S(1)}, s32[8]{0:T(128)}, u32[]{:S(2)}) copy-start(s32[8]{0:T(128)} %constant.25.clone) | copy-start | bytes 100
  0.0 0.9 %copy-start.6 = (s32[1,16384]{1,0:T(1,128)S(1)}, s32[1,16384]{1,0:T(1,128)}, u32[]{:S(2)}) copy-start(s32[1,16384]{1,0:T(1,128)} %cell_ref.2) | copy-start | bytes 196612
  0.9 0.8 %copy-start.7 = (bf16[1,16384]{1,0:T(2,128)(2,1)S(1)}, bf16[1,16384]{1,0:T(2,128)(2,1)}, u32[]{:S(2)}) copy-start(bf16[1,16384]{1,0:T(2,128)(2,1)} %charge_ref.1) | copy-start | bytes 98308
  4.1 1.9 %collective-permute-start = (f32[256,256]{1,0:T(8,128)S(1)}, f32[256,256]{1,0:T(8,128)S(1)}, u32[]{:S(2)}, u32[]{:S(2)}) collective-permute-start(f32[256,256]{1,0:T(8,128)S(1)} %deposit.1), channel_id=1, source_target_pairs={{0,1},{1,0},{2,3},{3,2},{4,5},{5,4},{6,7},{7,6},{8,9},{9,8},{10,11... | collective-permute-start | bytes 786440 | tf_op jit(solution)/shard_map/ppermute | solution.py:296
  6.0 11.1 %collective-permute-start.1 = (f32[256,256]{1,0:T(8,128)S(1)}, f32[256,256]{1,0:T(8,128)S(1)}, u32[]{:S(2)}, u32[]{:S(2)}) collective-permute-start(f32[256,256]{1,0:T(8,128)S(1)} %get-tuple-element.6), channel_id=1, source_target_pairs={{6,1},{1,6},{8,3},{3,8},{10,5},{5,10},{12,7},{7,12},{14,9},{9,14},... | collective-permute-start | bytes 786440 | tf_op jit(solution)/shard_map/ppermute | solution.py:303
  10.5 7.8 %collective-permute-start.2 = (f32[256,256]{1,0:T(8,128)S(1)}, f32[256,256]{1,0:T(8,128)S(1)}, u32[]{:S(2)}, u32[]{:S(2)}) collective-permute-start(f32[256,256]{1,0:T(8,128)S(1)} %get-tuple-element.6), channel_id=1, source_target_pairs={{4,1},{1,4},{6,3},{3,6},{8,5},{5,8},{10,7},{7,10},{12,9},{9,12},{1... | collective-permute-start | bytes 786440 | tf_op jit(solution)/shard_map/ppermute | solution.py:303
  12.4 9.6 %collective-permute-start.3 = (f32[256,256]{1,0:T(8,128)S(1)}, f32[256,256]{1,0:T(8,128)S(1)}, u32[]{:S(2)}, u32[]{:S(2)}) collective-permute-start(f32[256,256]{1,0:T(8,128)S(1)} %get-tuple-element.6), channel_id=1, source_target_pairs={{2,1},{1,2},{4,3},{3,4},{6,5},{5,6},{8,7},{7,8},{10,9},{9,10},{12,... | collective-permute-start | bytes 786440 | tf_op jit(solution)/shard_map/ppermute | solution.py:303
  22.1 4.4 %copy-start = (bf16[192,256]{1,0:T(8,128)(2,1)S(1)}, bf16[192,256]{1,0:T(8,128)(2,1)}, u32[]{:S(2)}) copy-start(bf16[192,256]{1,0:T(8,128)(2,1)} %constant.26.clone.z_ref) | copy-start | bytes 294916
  22.1 4.4 %copy-start.1 = (bf16[128,192]{1,0:T(8,128)(2,1)S(1)}, bf16[128,192]{1,0:T(8,128)(2,1)}, u32[]{:S(2)}) copy-start(bf16[128,192]{1,0:T(8,128)(2,1)} %constant.27.clone.x_ref) | copy-start | bytes 147460
  22.2 4.4 %copy-start.2 = (bf16[2,64,192]{2,1,0:T(8,128)(2,1)S(1)}, bf16[2,64,192]{2,1,0:T(8,128)(2,1)}, u32[]{:S(2)}) copy-start(bf16[2,64,192]{2,1,0:T(8,128)(2,1)} %constant.28.clone.y_ref) | copy-start | bytes 147460
  22.2 4.4 %copy-start.3 = (bf16[256,128]{1,0:T(8,128)(2,1)S(1)}, bf16[256,128]{1,0:T(8,128)(2,1)}, u32[]{:S(2)}) copy-start(bf16[256,128]{1,0:T(8,128)(2,1)} %constant.29.clone.iz_hi_ref) | copy-start | bytes 196612
  22.2 4.4 %copy-start.4 = (bf16[256,128]{1,0:T(8,128)(2,1)S(1)}, bf16[256,128]{1,0:T(8,128)(2,1)}, u32[]{:S(2)}) copy-start(bf16[256,128]{1,0:T(8,128)(2,1)} %constant.30.clone.iz_lo_ref) | copy-start | bytes 196612
  22.2 4.4 %copy-start.8 = (bf16[2,64,96]{2,1,0:T(8,128)(2,1)S(1)}, bf16[2,64,96]{2,1,0:T(8,128)(2,1)}, u32[]{:S(2)}) copy-start(bf16[2,64,96]{2,1,0:T(8,128)(2,1)} %constant.31.clone.iy_ref) | copy-start | bytes 73732
  22.2 4.3 %copy-start.9 = (bf16[64,192]{1,0:T(8,128)(2,1)S(1)}, bf16[64,192]{1,0:T(8,128)(2,1)}, u32[]{:S(2)}) copy-start(bf16[64,192]{1,0:T(8,128)(2,1)} %constant.32.clone.ix_ref) | copy-start | bytes 73732
  22.2 4.2 %collective-permute-start.4 = (f32[3,256,256]{2,1,0:T(8,128)S(1)}, f32[3,256,256]{2,1,0:T(8,128)S(1)}, u32[]{:S(2)}, u32[]{:S(2)}) collective-permute-start(f32[3,256,256]{2,1,0:T(8,128)S(1)} %pad_maximum_fusion), channel_id=1, source_target_pairs={{0,1},{1,0},{2,3},{3,2},{4,5},{5,4},{6,7},{7,6},{8,9},{9,8},{10,11... | collective-permute-start | bytes 2359304 | tf_op jit(solution)/shard_map/ppermute | solution.py:305
  26.6 18.0 %copy-start.5 = (s32[1,16384]{1,0:T(1,128)S(1)}, s32[1,16384]{1,0:T(1,128)}, u32[]{:S(2)}) copy-start(s32[1,16384]{1,0:T(1,128)} %cell_ref.3) | copy-start | bytes 196612
  42.9 1.6 %collective-permute-start.5 = (f32[512,128]{1,0:T(8,128)S(1)}, f32[512,128]{1,0:T(8,128)S(1)}, u32[]{:S(2)}, u32[]{:S(2)}) collective-permute-start(f32[512,128]{1,0:T(8,128)S(1)} %spectral.1.own_ref), channel_id=1, source_target_pairs={{0,1},{1,0},{2,3},{3,2},{4,5},{5,4},{6,7},{7,6},{8,9},{9,8},{10,11... | collective-permute-start | bytes 786440 | tf_op jit(solution)/shard_map/ppermute | solution.py:312

commit v2 on v1

v2 whole, which is shorter than its diff:
```python
import functools

import jax
import jax.numpy as jnp
import numpy as np
from jax import lax
from jax.experimental import pallas as pl
from jax.experimental.pallas import tpu as pltpu
from jax.sharding import PartitionSpec as P

GX = 32
GY = 32
GZ = 64
SPAN = 3
MX = 64
MY = 64
MZ = 128
BF16 = jnp.bfloat16
F32 = jnp.float32
CHARGE_BITS = 12
CHARGE_UNITS = 512.0
GATHER_CHUNK = 512
PITCH_X = 2 * MX + 1
PITCH_Y = GY + 1
KX_BLOCK = 16
VMEM_LIMIT = 36 * 2**20
STAGE_FLOPS = 2 * 3 * (1024 * 64 * 256 + 2 * 2048 * 64 * 64)


def hi_lo(table):
    top = table.astype(np.float32).astype(BF16)
    rest = (table - top.astype(np.float64)).astype(np.float32).astype(BF16)
    return top, rest


def stacked_terms(table):
    top, rest = hi_lo(table)
    return np.concatenate([top, top, rest], axis=-1)


def phases(rows, columns, period):
    angles = 2.0 * np.pi / period * ((rows[:, None] * columns[None, :]) % period)
    return np.cos(angles), np.sin(angles)


def make_tables(pencils):
    width = MY // pencils
    cos_z, sin_z = phases(np.arange(GZ), np.arange(MZ), MZ)
    forward_z = np.concatenate([cos_z, -sin_z], axis=1)
    grid_x = (np.arange(8)[None, :] * 4 + np.arange(4)[:, None]).reshape(-1)
    cos_x, sin_x = phases(np.arange(MX), grid_x, MX)
    forward_x = np.block([[cos_x, sin_x], [-sin_x, cos_x]])
    forward_y = []
    inverse_y = []
    for pencil in range(pencils):
        own = np.arange(pencil * width, (pencil + 1) * width)
        cos_y, sin_y = phases(own, np.arange(GY), MY)
        forward_y.append(stacked_terms(np.block([[cos_y, sin_y], [-sin_y, cos_y]])))
        inverse_y.append(stacked_terms(np.concatenate([cos_y.T, sin_y.T], axis=0)))
    cos_b, sin_b = phases(np.arange(MZ), np.arange(GZ), MZ)
    inverse_z = np.block([[cos_b, sin_b], [-sin_b, cos_b]])
    cos_c, sin_c = phases(np.arange(GX), np.arange(MX), MX)
    inverse_x = np.concatenate([cos_c, sin_c], axis=0) / float(MX * MY * MZ)
    tables = dict(
        z=stacked_terms(forward_z.T).T,
        x=stacked_terms(forward_x),
        y=np.concatenate(forward_y),
        iz=np.concatenate(hi_lo(inverse_z), axis=1),
        iy=np.concatenate(inverse_y),
        ix=stacked_terms(inverse_x),
    )
    places = {}
    packed = []
    at = 0
    for name, table in tables.items():
        rows, columns = table.shape
        places[name] = (at, rows // (pencils if name in ("y", "iy") else 1), columns)
        packed.append(np.pad(table, ((0, 0), (0, 256 - columns))))
        at += rows
    return np.concatenate(packed), places


def in_hbm(array):
    return pltpu.with_memory_space_constraint(array, pltpu.HBM)


def in_vmem(array):
    return pltpu.with_memory_space_constraint(array, pltpu.VMEM)


def dot(a, b):
    return jnp.dot(a, b, preferred_element_type=F32)


def split(value):
    top = value.astype(BF16)
    return top, (value - top.astype(F32)).astype(BF16)


def data_terms(value):
    top, rest = split(value)
    return jnp.concatenate([top, rest, top], axis=0)


def one_hot(index, rows, value):
    place = lax.broadcasted_iota(jnp.int16, (rows, index.shape[1]), 0)
    return jnp.where(place == index.astype(jnp.int16), value, jnp.zeros((), BF16))


def deposit_kernel(particles_ref, table_hbm, out_ref, table_ref, arrived):
    copy = pltpu.make_async_copy(table_hbm, table_ref, arrived)
    copy.start()
    particles = particles_ref[...]
    cell = particles >> CHARGE_BITS
    charge = (particles & (2**CHARGE_BITS - 1)).astype(F32) * (1.0 / CHARGE_UNITS)
    row = ((cell >> 6) & 31) * 8 + (cell >> 13)
    column = ((cell >> 11) & 3) * 64 + (cell & 63)
    out_ref[...] = lax.dot_general(
        one_hot(row, 256, jnp.ones((), BF16)),
        one_hot(column, 256, charge.astype(BF16)),
        (((1,), (1,)), ((), ())),
        preferred_element_type=F32,
    )
    copy.wait()


def deposit(cells, charge, packed):
    units = (charge.astype(F32) * CHARGE_UNITS).astype(jnp.int32)
    particles = (cells << CHARGE_BITS) + units
    return pl.pallas_call(
        deposit_kernel,
        in_specs=[
            pl.BlockSpec(memory_space=pltpu.VMEM),
            pl.BlockSpec(memory_space=pltpu.HBM),
        ],
        out_specs=[pl.BlockSpec(memory_space=pltpu.VMEM)] * 2,
        out_shape=[
            jax.ShapeDtypeStruct((256, 256), F32),
            jax.ShapeDtypeStruct(packed.shape, packed.dtype),
        ],
        scratch_shapes=[pltpu.SemaphoreType.DMA],
        compiler_params=pltpu.CompilerParams(vmem_limit_bytes=VMEM_LIMIT),
        name="deposit",
    )(in_vmem(particles), in_hbm(jnp.asarray(packed)))


def table_rows(table_ref, places, name, pencil=None):
    start, rows, columns = places[name]
    if pencil is not None:
        start = pl.multiple_of(start + pencil * rows, 16)
    return table_ref[pl.ds(start, rows), :columns]


def stage_zx(density, table_z, table_x, after_z, after_x, at):
    top, rest = split(density)
    for low in range(4):
        lanes = slice(low * GZ, (low + 1) * GZ)
        terms = jnp.concatenate([top[:, lanes], rest[:, lanes], top[:, lanes]], axis=1)
        after_z[:, 2 * MZ * low : 2 * MZ * (low + 1)] = dot(terms, table_z)
    for pair in range(GY // 2):
        sides = []
        for y in (2 * pair, 2 * pair + 1):
            tiles = [
                after_z[8 * y : 8 * y + 8, (2 * low + part) * MZ : (2 * low + part + 1) * MZ]
                for part in range(2)
                for low in range(4)
            ]
            sides.append(jnp.concatenate(tiles, axis=0))
        out = dot(table_x, data_terms(jnp.concatenate(sides, axis=1)))
        for side in range(2):
            rows = pl.ds((2 * pair + side) * PITCH_X, 2 * MX)
            after_x[at, rows, :] = out[:, side * MZ : (side + 1) * MZ]


def spectral_kernel(places, offsets, first, last, *refs):
    refs = list(refs)
    count = len(offsets)
    densities = [refs.pop(0) for _ in range(count)]
    green_ref = refs.pop(0)
    table_ref = refs.pop(0)
    before_ref = None if first else refs.pop(0)
    out_ref = refs.pop(0)
    after_z = refs.pop(0)
    after_x = refs.pop(0)
    green = refs.pop(0)
    arrived = refs.pop(0)
    total, back = (refs.pop(0), refs.pop(0)) if last else (out_ref, None)
    width = green_ref.shape[3]
    block = KX_BLOCK
    pencil = lax.axis_index("pencil")
    sign = 1 - 2 * pencil

    def copy(at, step):
        kx = pl.ds(step * block, block)
        return pltpu.make_async_copy(
            green_ref.at[SPAN + sign * offsets[at], :, kx], green.at[at, :, kx], arrived.at[at, step]
        )

    for step in range(MX // block):
        for at in range(count):
            copy(at, step).start()

    def table(name):
        return table_rows(table_ref, places, name, pencil if name in ("y", "iy") else None)

    for at, density_ref in enumerate(densities):
        stage_zx(density_ref[...], table("z"), table("x"), after_z, after_x, at)

    def kx_block(step):
        for at in range(count):
            copy(at, step).wait()
        for pair in range(block // 2):
            sums = [[None, None], [None, None]]
            starts = [
                pl.multiple_of((step * block + 2 * pair + side) * width, width) for side in range(2)
            ]
            if not first:
                for side in range(2):
                    rows = pl.ds(starts[side], width)
                    sums[side] = [before_ref[rows, :MZ], before_ref[rows, MZ:]]
            for at in range(count):
                sides = []
                for side in range(2):
                    kx = step * block + 2 * pair + side
                    real = after_x[at, pl.ds(kx, GY, stride=PITCH_X), :]
                    imag = after_x[at, pl.ds(MX + kx, GY, stride=PITCH_X), :]
                    sides.append(jnp.concatenate([real, imag], axis=0))
                out = dot(table("y"), data_terms(jnp.concatenate(sides, axis=1)))
                for side in range(2):
                    kx = step * block + 2 * pair + side
                    real = out[:width, side * MZ : (side + 1) * MZ]
                    imag = out[width:, side * MZ : (side + 1) * MZ]
                    green_real = green[at, 0, kx]
                    green_imag = green[at, 1, kx]
                    terms = (
                        green_real * real - green_imag * imag,
                        green_real * imag + green_imag * real,
                    )
                    for part in range(2):
                        held = sums[side][part]
                        sums[side][part] = terms[part] if held is None else held + terms[part]
            for side in range(2):
                rows = pl.ds(starts[side], width)
                total[rows, :MZ] = sums[side][0]
                total[rows, MZ:] = sums[side][1]

    pl.loop(0, MX // block)(kx_block)
    if not last:
        return

    lane = lax.broadcasted_iota(jnp.int32, (GY, 2 * GZ), 1)
    front = lane < GZ

    lane = lax.broadcasted_iota(jnp.int32, (GY, 2 * GZ), 1)
    front = lane < GZ
    def back_block(step):
        start = pl.multiple_of(step * block * width, block * width)
        top, rest = split(total[pl.ds(start, block * width), :])
        both = table("iz")
        wide = dot(top, both)
        turned = wide[:, : 2 * GZ] + (wide[:, 2 * GZ :] + dot(rest, both[:, : 2 * GZ]))
        for pair in range(block // 2):
            sides = [
                turned[(2 * pair + side) * width : (2 * pair + side + 1) * width, :]
                for side in range(2)
            ]
            out = dot(table("iy"), data_terms(jnp.concatenate(sides, axis=1)))
            for side in range(2):
                kx = step * block + 2 * pair + side
                by_cos = out[:GY, side * 2 * GZ : (side + 1) * 2 * GZ]
                by_sin = pltpu.roll(out[GY:, side * 2 * GZ : (side + 1) * 2 * GZ], GZ, 1)
                back[pl.ds(kx * PITCH_Y, GY), :] = by_cos + jnp.where(front, -by_sin, by_sin)

    pl.loop(0, MX // block)(back_block)
    for pair in range(GY // 2):
        sides = [back[pl.ds(2 * pair + side, MX, stride=PITCH_Y), :] for side in range(2)]
        out = dot(table("ix"), data_terms(jnp.concatenate(sides, axis=1)))
        even = out[:GX, : 2 * GZ] - pltpu.roll(out[GX:, : 2 * GZ], GZ, 1)
        odd = pltpu.roll(out[:GX, 2 * GZ :], GZ, 1) - out[GX:, 2 * GZ :]
        out_ref[pair * GX : (pair + 1) * GX, :] = jnp.where(front, even, odd)


def spectral(offsets, densities, green, tables, before, last):
    count = len(densities)
    first = before is None
    width = green.shape[3]
    packed, places = tables
    scratch = [
        pltpu.VMEM((256, 1024), F32),
        pltpu.VMEM((count, GY * PITCH_X, MZ), F32),
        pltpu.VMEM((count,) + green.shape[1:], F32),
        pltpu.SemaphoreType.DMA((count, MX // KX_BLOCK)),
    ]
    out_shape = jax.ShapeDtypeStruct((MX * width, 2 * MZ), F32)
    if last:
        scratch.append(pltpu.VMEM((MX * width, 2 * MZ), F32))
        scratch.append(pltpu.VMEM((MX * PITCH_Y, 2 * GZ), F32))
        out_shape = jax.ShapeDtypeStruct((512, 128), F32)
    vmem = pl.BlockSpec(memory_space=pltpu.VMEM)
    return pl.pallas_call(
        functools.partial(spectral_kernel, places, offsets, first, last),
        in_specs=[
            *([vmem] * count),
            pl.BlockSpec(memory_space=pltpu.HBM),
            vmem,
            *([] if first else [vmem]),
        ],
        out_specs=vmem,
        scratch_shapes=scratch,
        out_shape=out_shape,
        compiler_params=pltpu.CompilerParams(vmem_limit_bytes=VMEM_LIMIT),
        cost_estimate=pl.CostEstimate(
            flops=2 * count * STAGE_FLOPS, bytes_accessed=count * 2**21, transcendentals=0
        ),
        name="spectral_last" if last else "spectral_part",
    )(
        *map(in_vmem, densities),
        in_hbm(green),
        in_vmem(packed),
        *([] if first else [in_vmem(before)]),
    )


def gather_kernel(own_ref, other_ref, cell_ref, out_ref, field):
    potential = own_ref[...] + other_ref[...]
    lane = lax.broadcasted_iota(jnp.int32, (512, 128), 1)
    row = lax.broadcasted_iota(jnp.int32, (512, 128), 0)
    x = row % GX
    z = lane % GZ
    zero = jnp.zeros((GX, 128), F32)
    below = jnp.where(x == 0, 0.0, pltpu.roll(potential, 1, 0))
    above = jnp.where(x == GX - 1, 0.0, pltpu.roll(potential, 511, 0))
    field_x = 0.5 * (below - above)
    turned = pltpu.roll(potential, GZ, 1)
    before = jnp.concatenate([zero, turned[: 512 - GX]], axis=0)
    after = jnp.concatenate([turned[GX:], zero], axis=0)
    field_y = 0.5 * (
        jnp.where(lane < GZ, before, turned) - jnp.where(lane < GZ, turned, after)
    )
    left = jnp.where(z == 0, 0.0, pltpu.roll(potential, 1, 1))
    right = jnp.where(z == GZ - 1, 0.0, pltpu.roll(potential, 127, 1))
    field_z = 0.5 * (left - right)
    for part, value in enumerate((field_x, field_y, field_z)):
        field[part * 128 : (part + 1) * 128, :] = jnp.transpose(value).astype(BF16)

    count = cell_ref.shape[1]
    chunk = min(GATHER_CHUNK, count)
    for at in range(0, count, chunk):
        cell = cell_ref[:, at : at + chunk]
        y = (cell >> 6) & 31
        high = (y >> 1) * GX + (cell >> 11)
        low = (y & 1) * GZ + (cell & 63)
        picked = dot(field[...], one_hot(high, 512, jnp.ones((), BF16)))
        inside = lax.broadcasted_iota(jnp.int32, (128, chunk), 0) == low
        for part in range(3):
            values = jnp.where(inside, picked[part * 128 : (part + 1) * 128], 0.0)
            out_ref[part, :, at : at + chunk] = jnp.sum(values, axis=0, keepdims=True)


def gather(own, other, cells):
    return pl.pallas_call(
        gather_kernel,
        out_shape=jax.ShapeDtypeStruct((3, 1, cells.shape[1]), F32),
        scratch_shapes=[pltpu.VMEM((384, 512), BF16)],
        compiler_params=pltpu.CompilerParams(vmem_limit_bytes=48 * 2**20),
        name="gather",
    )(own, other, cells)


def per_device(tables, charge, cell_deposit, cell_gather, green_spectra):
    pencils = lax.axis_size("pencil")
    bunches = lax.axis_size("bunch")
    swap = [(i, (i + 1) % pencils) for i in range(pencils)]
    packed, places = tables
    part, packed = deposit(cell_deposit, charge, packed)
    tables = (packed, places)
    density = part + lax.ppermute(part, "pencil", swap)
    near = []
    for distance in range(SPAN, 0, -1):
        route = []
        for bunch in range(distance, bunches):
            ends = (bunch * pencils, (bunch - distance) * pencils + 1)
            route.extend([ends, ends[::-1]])
        near.append(lax.ppermute(density, ("bunch", "pencil"), route))
    steps = tuple(range(SPAN, 0, -1))
    back_steps = tuple(-step for step in steps)

    def terms(offsets, densities, before, last):
        return spectral(offsets, densities, green_spectra, tables, before, last)

    total = terms((0,), [density], None, False)
    total, near[0] = lax.optimization_barrier((total, near[0]))
    far = [lax.ppermute(each, "pencil", swap) for each in near[:-1]]
    total = terms(steps[:-1], near[:-1], total, False)
    total, near[-1] = lax.optimization_barrier((total, near[-1]))
    far.append(lax.ppermute(near[-1], "pencil", swap))
    total = terms(steps[-1:], near[-1:], total, False)
    own = terms(back_steps, far, total, True)
    other = lax.ppermute(own, "pencil", swap)
    return gather(own, other, cell_gather)


def solution(mesh):
    in_specs = (
        P(("groups", "bunch"), "pencil"),
        P(("groups", "bunch"), "pencil"),
        P(("groups", "bunch"), "pencil"),
        P(None, None, None, "pencil", None),
    )
    out_specs = P(None, ("groups", "bunch"), "pencil")
    tables = make_tables(mesh.shape["pencil"])
    return jax.shard_map(
        functools.partial(per_device, tables),
        mesh=mesh,
        in_specs=in_specs,
        out_specs=out_specs,
        check_vma=False,
    )
```

time: 53.4 us -> 45.6 us (0.85)
  waiting for transfers between devices: 10.2 us -> 2.7 us
  local copies, waits for them, and re-layouts: 1.87 us -> 0.01 us
  other arithmetic: 0.09 us -> 1.01 us
    ppermute x3, waiting for transfers between devices: 6.1 us -> 0.01 us  [per_device(): near.append(lax.ppermute(density, ('bunch', 'pencil'), route))]
    unnamed x27 -> x2, local copies, waits for them, and re-layouts: 1.82 us -> 0.01 us
    ppermute x1 -> x3, waiting for transfers between devices: 1.82 us -> 0.01 us  [the longest x2 0.01 us: per_device(): far = [lax.ppermute(each, 'pencil', swap) for each in near[:-1]]]
    add x0 -> x2, other arithmetic: none -> 1.01 us  [the longest x1 0.98 us: deposit(): particles = (cells << CHARGE_BITS) + units]
    ppermute x1 -> x3, starting transfers between devices: 2.3 us -> 2.71 us  [the longest x1 2.2 us: per_device(): far.append(lax.ppermute(near[-1], 'pencil', swap))]
    pallas_call x2 -> x5, Pallas kernels: 18.7 us -> 19 us  [the longest x4 16.6 us: spectral(): pl.pallas_call(functools.partial(spectral_kernel, places, offsets, first,...]
  transfers between devices with their start and end apart: 6 -> 8, of which waited for: 6 -> 2; matrix products, arithmetic and copies ran while one was open for 0% -> 0% of each run, Pallas kernels for 0% -> 19%
where the time goes in v2:
time: 45.6 us; the launch traced here: 44.9 us
  Pallas kernels  27.6 us (61%)
  starting transfers between devices  13.4 us (29%)
  waiting for transfers between devices  2.7 us (6%)
  other arithmetic  1.01 us (2%)
    pallas_call x4, Pallas kernels, spectral(): pl.pallas_call(functools.partial(spectral_kernel, places, offsets, first,...  16.6 us
    ppermute x3, starting transfers between devices, per_device(): near.append(lax.ppermute(density, ('bunch', 'pencil'), route))  9.93 us
    pallas_call x1, Pallas kernels, gather(): pl.pallas_call(gather_kernel, out_shape=jax.ShapeDtypeStruct((3, 1, cells...  8.58 us
    pallas_call x1, Pallas kernels, deposit(): pl.pallas_call(deposit_kernel, in_specs=[pl.BlockSpec(memory_space=pltpu....  2.38 us
    ppermute x1, starting transfers between devices, per_device(): far.append(lax.ppermute(near[-1], 'pencil', swap))  2.2 us
    ppermute x1, waiting for transfers between devices, per_device(): other = lax.ppermute(own, 'pencil', swap)  1.52 us
    ppermute x1, waiting for transfers between devices, per_device(): density = part + lax.ppermute(part, 'pencil', swap)  1.16 us
    add x1, other arithmetic, deposit(): particles = (cells << CHARGE_BITS) + units  0.98 us
  transfers between devices with their start and end apart: 8, of which 2 were waited for; matrix products, arithmetic and copies ran while one was open for 0% of the time, Pallas kernels for 19%

profile of v2, /device:TPU:17, one launch (start us, length us, event | category | flops | bytes accessed | tf_op | source)
XLA Modules:
  0.0 44.9 jit_solution(5194779322076625094)
XLA Ops:
  0.0 1.0 %convert_add_fusion.particles_ref = s32[1,16384]{1,0:T(1,128)S(1)} fusion(bf16[1,16384]{1,0:T(2,128)(2,1)} %param.5, s32[1,16384]{1,0:T(1,128)} %param.6), kind=kLoop, calls=%fused_computation | loop fusion | flops 81920 | bytes 163840 | tf_op jit(solution)/shard_map/add | solution.py:129
  1.0 2.4 %deposit.1 = (f32[256,256]{1,0:T(8,128)S(1)}, bf16[896,256]{1,0:T(8,128)(2,1)S(1)}) custom-call(s32[1,16384]{1,0:T(1,128)S(1)} %convert_add_fusion.particles_ref, bf16[896,256]{1,0:T(8,128)(2,1)} %constant.6.clone.table_hbm), custom_call_target="tpu_custom_call" | custom-call | tf_op jit(solution)/shard_map/deposit/pallas_call | solution.py:130
  3.4 0.7 %collective-permute-start = (f32[256,256]{1,0:T(8,128)S(1)}, f32[256,256]{1,0:T(8,128)S(1)}, u32[]{:S(2)}, u32[]{:S(2)}) collective-permute-start(f32[256,256]{1,0:T(8,128)S(1)} %get-tuple-element.11), channel_id=1, source_target_pairs={{0,1},{1,0},{2,3},{3,2},{4,5},{5,4},{6,7},{7,6},{8,9},{9,8},{10,11... | collective-permute-start | bytes 786440 | tf_op jit(solution)/shard_map/ppermute | solution.py:377
  4.1 1.2 %collective-permute-done = f32[256,256]{1,0:T(8,128)S(1)} collective-permute-done((f32[256,256]{1,0:T(8,128)S(1)}, f32[256,256]{1,0:T(8,128)S(1)}, u32[]{:S(2)}, u32[]{:S(2)}) %collective-permute-start) | collective-permute-done | bytes 262176 | tf_op jit(solution)/shard_map/ppermute | solution.py:377
  5.3 4.4 %collective-permute-start.1 = (f32[256,256]{1,0:T(8,128)S(1)}, f32[256,256]{1,0:T(8,128)S(1)}, u32[]{:S(2)}, u32[]{:S(2)}) collective-permute-start(f32[256,256]{1,0:T(8,128)S(1)} %add.7.refs_0_), channel_id=1, source_target_pairs={{6,1},{1,6},{8,3},{3,8},{10,5},{5,10},{12,7},{7,12},{14,9},{9,14},... | collective-permute-start | bytes 786440 | tf_op jit(solution)/shard_map/ppermute | solution.py:384
  9.7 2.0 %collective-permute-start.3 = (f32[256,256]{1,0:T(8,128)S(1)}, f32[256,256]{1,0:T(8,128)S(1)}, u32[]{:S(2)}, u32[]{:S(2)}) collective-permute-start(f32[256,256]{1,0:T(8,128)S(1)} %add.7.refs_0_), channel_id=1, source_target_pairs={{4,1},{1,4},{6,3},{3,6},{8,5},{5,8},{10,7},{7,10},{12,9},{9,12},{1... | collective-permute-start | bytes 786440 | tf_op jit(solution)/shard_map/ppermute | solution.py:384
  11.7 3.5 %collective-permute-start.5 = (f32[256,256]{1,0:T(8,128)S(1)}, f32[256,256]{1,0:T(8,128)S(1)}, u32[]{:S(2)}, u32[]{:S(2)}) collective-permute-start(f32[256,256]{1,0:T(8,128)S(1)} %add.7.refs_0_), channel_id=1, source_target_pairs={{2,1},{1,2},{4,3},{3,4},{6,5},{5,6},{8,7},{7,8},{10,9},{9,10},{12,... | collective-permute-start | bytes 786440 | tf_op jit(solution)/shard_map/ppermute | solution.py:384
  15.3 2.3 %spectral_part.3.refs_4_ = f32[2048,256]{1,0:T(8,128)S(1)} custom-call(f32[256,256]{1,0:T(8,128)S(1)} %add.7.refs_0_, f32[7,2,64,32,128]{4,3,2,1,0:T(8,128)} %refs_3_.1, bf16[896,256]{1,0:T(8,128)(2,1)S(1)} %get-tuple-element.12.refs_2_.refs_3_.refs_4_), custom_call_target="tpu_custom_call" | custom-call | flops 402653184 | bytes 2097152 | tf_op jit(solution)/shard_map/spectral_part/pallas_call | solution.py:300
  17.6 0.0 collective-permute-done.1.refs_0_
  17.6 0.0 collective-permute-done.3.refs_1_
  17.6 3.8 %spectral_part.4.refs_3_ = f32[2048,256]{1,0:T(8,128)S(1)} custom-call(f32[256,256]{1,0:T(8,128)S(1)} %collective-permute-done.1.refs_0_, f32[256,256]{1,0:T(8,128)S(1)} %collective-permute-done.3.refs_1_, f32[7,2,64,32,128]{4,3,2,1,0:T(8,128)} %refs_3_.1, bf16[896,256]{1,0:T(8,128)(2,1)S(1)} %get-tuple-element.12.refs_2_.refs_3_.refs_4_, ...), custom_call_target="tpu_custom_call" | custom-call | flops 805306368 | bytes 4194304 | tf_op jit(solution)/shard_map/spectral_part/pallas_call | solution.py:300
  21.4 0.0 collective-permute-done.5.refs_0_
  21.4 2.2 %collective-permute-start.6 = (f32[256,256]{1,0:T(8,128)S(1)}, f32[256,256]{1,0:T(8,128)S(1)}, u32[]{:S(2)}, u32[]{:S(2)}) collective-permute-start(f32[256,256]{1,0:T(8,128)S(1)} %collective-permute-done.5.refs_0_), channel_id=1, source_target_pairs={{0,1},{1,0},{2,3},{3,2},{4,5},{5,4},{6,7},{7,6},{8,9},{9,8},{10,11... | collective-permute-start | bytes 786440 | tf_op jit(solution)/shard_map/ppermute | solution.py:396
  23.6 0.0 collective-permute-start.2
  23.6 0.5 %collective-permute-start.4 = (f32[256,256]{1,0:T(8,128)S(1)}, f32[256,256]{1,0:T(8,128)S(1)}, u32[]{:S(2)}, u32[]{:S(2)}) collective-permute-start(f32[256,256]{1,0:T(8,128)S(1)} %collective-permute-done.3.refs_1_), channel_id=1, source_target_pairs={{0,1},{1,0},{2,3},{3,2},{4,5},{5,4},{6,7},{7,6},{8,9},{9,8},{10,11... | collective-permute-start | bytes 786440 | tf_op jit(solution)/shard_map/ppermute | solution.py:393
  24.1 2.3 %spectral_part.5.refs_5_ = f32[2048,256]{1,0:T(8,128)S(1)} custom-call(f32[256,256]{1,0:T(8,128)S(1)} %collective-permute-done.5.refs_0_, f32[7,2,64,32,128]{4,3,2,1,0:T(8,128)} %refs_3_.1, bf16[896,256]{1,0:T(8,128)(2,1)S(1)} %get-tuple-element.12.refs_2_.refs_3_.refs_4_, f32[2048,256]{1,0:T(8,128)S(1)} %spectral_part.4.refs_3_), custom_call_target="tpu_custom_call" | custom-call | flops 402653184 | bytes 2097152 | tf_op jit(solution)/shard_map/spectral_part/pallas_call | solution.py:300
  26.4 0.0 copy-start
  26.5 0.0 collective-permute-done.6.refs_2_
  26.5 0.0 collective-permute-done.2.refs_0_
  26.5 0.0 collective-permute-done.4.refs_1_
  26.5 8.2 %spectral_last.1.own_ref = f32[512,128]{1,0:T(8,128)S(1)} custom-call(f32[256,256]{1,0:T(8,128)S(1)} %collective-permute-done.2.refs_0_, f32[256,256]{1,0:T(8,128)S(1)} %collective-permute-done.4.refs_1_, f32[256,256]{1,0:T(8,128)S(1)} %collective-permute-done.6.refs_2_, f32[7,2,64,32,128]{4,3,2,1,0:T(8,128)} %refs_3_.1, ...), custom_call_target="tpu_custom_call" | custom-call | flops 1207959552 | bytes 6291456 | tf_op jit(solution)/shard_map/spectral_last/pallas_call | solution.py:300
  34.7 0.1 collective-permute-start.7
  34.8 1.5 %collective-permute-done.7.other_ref = f32[512,128]{1,0:T(8,128)S(1)} collective-permute-done((f32[512,128]{1,0:T(8,128)S(1)}, f32[512,128]{1,0:T(8,128)S(1)}, u32[]{:S(2)}, u32[]{:S(2)}) %collective-permute-start.7) | collective-permute-done | bytes 262176 | tf_op jit(solution)/shard_map/ppermute | solution.py:399
  36.3 0.0 copy-done
  36.3 8.6 %gather.1 = f32[3,1,16384]{2,1,0:T(1,128)} custom-call(f32[512,128]{1,0:T(8,128)S(1)} %spectral_last.1.own_ref, f32[512,128]{1,0:T(8,128)S(1)} %collective-permute-done.7.other_ref, s32[1,16384]{1,0:T(1,128)S(1)} %copy-done), custom_call_target="tpu_custom_call" | custom-call | tf_op jit(solution)/shard_map/gather/pallas_call | solution.py:361
  (1 shorter events, 0.0 us)
Async XLA Ops:
  3.4 1.9 %collective-permute-start = (f32[256,256]{1,0:T(8,128)S(1)}, f32[256,256]{1,0:T(8,128)S(1)}, u32[]{:S(2)}, u32[]{:S(2)}) collective-permute-start(f32[256,256]{1,0:T(8,128)S(1)} %get-tuple-element.11), channel_id=1, source_target_pairs={{0,1},{1,0},{2,3},{3,2},{4,5},{5,4},{6,7},{7,6},{8,9},{9,8},{10,11... | collective-permute-start | bytes 786440 | tf_op jit(solution)/shard_map/ppermute | solution.py:377
  5.3 12.3 %collective-permute-start.1 = (f32[256,256]{1,0:T(8,128)S(1)}, f32[256,256]{1,0:T(8,128)S(1)}, u32[]{:S(2)}, u32[]{:S(2)}) collective-permute-start(f32[256,256]{1,0:T(8,128)S(1)} %add.7.refs_0_), channel_id=1, source_target_pairs={{6,1},{1,6},{8,3},{3,8},{10,5},{5,10},{12,7},{7,12},{14,9},{9,14},... | collective-permute-start | bytes 786440 | tf_op jit(solution)/shard_map/ppermute | solution.py:384
  9.7 7.9 %collective-permute-start.3 = (f32[256,256]{1,0:T(8,128)S(1)}, f32[256,256]{1,0:T(8,128)S(1)}, u32[]{:S(2)}, u32[]{:S(2)}) collective-permute-start(f32[256,256]{1,0:T(8,128)S(1)} %add.7.refs_0_), channel_id=1, source_target_pairs={{4,1},{1,4},{6,3},{3,6},{8,5},{5,8},{10,7},{7,10},{12,9},{9,12},{1... | collective-permute-start | bytes 786440 | tf_op jit(solution)/shard_map/ppermute | solution.py:384
  11.7 9.7 %collective-permute-start.5 = (f32[256,256]{1,0:T(8,128)S(1)}, f32[256,256]{1,0:T(8,128)S(1)}, u32[]{:S(2)}, u32[]{:S(2)}) collective-permute-start(f32[256,256]{1,0:T(8,128)S(1)} %add.7.refs_0_), channel_id=1, source_target_pairs={{2,1},{1,2},{4,3},{3,4},{6,5},{5,6},{8,7},{7,8},{10,9},{9,10},{12,... | collective-permute-start | bytes 786440 | tf_op jit(solution)/shard_map/ppermute | solution.py:384
  21.4 5.1 %collective-permute-start.6 = (f32[256,256]{1,0:T(8,128)S(1)}, f32[256,256]{1,0:T(8,128)S(1)}, u32[]{:S(2)}, u32[]{:S(2)}) collective-permute-start(f32[256,256]{1,0:T(8,128)S(1)} %collective-permute-done.5.refs_0_), channel_id=1, source_target_pairs={{0,1},{1,0},{2,3},{3,2},{4,5},{5,4},{6,7},{7,6},{8,9},{9,8},{10,11... | collective-permute-start | bytes 786440 | tf_op jit(solution)/shard_map/ppermute | solution.py:396
  23.6 2.9 %collective-permute-start.2 = (f32[256,256]{1,0:T(8,128)S(1)}, f32[256,256]{1,0:T(8,128)S(1)}, u32[]{:S(2)}, u32[]{:S(2)}) collective-permute-start(f32[256,256]{1,0:T(8,128)S(1)} %collective-permute-done.1.refs_0_), channel_id=1, source_target_pairs={{0,1},{1,0},{2,3},{3,2},{4,5},{5,4},{6,7},{7,6},{8,9},{9,8},{10,11... | collective-permute-start | bytes 786440 | tf_op jit(solution)/shard_map/ppermute | solution.py:393
  23.6 2.9 %collective-permute-start.4 = (f32[256,256]{1,0:T(8,128)S(1)}, f32[256,256]{1,0:T(8,128)S(1)}, u32[]{:S(2)}, u32[]{:S(2)}) collective-permute-start(f32[256,256]{1,0:T(8,128)S(1)} %collective-permute-done.3.refs_1_), channel_id=1, source_target_pairs={{0,1},{1,0},{2,3},{3,2},{4,5},{5,4},{6,7},{7,6},{8,9},{9,8},{10,11... | collective-permute-start | bytes 786440 | tf_op jit(solution)/shard_map/ppermute | solution.py:393
  26.4 9.9 %copy-start = (s32[1,16384]{1,0:T(1,128)S(1)}, s32[1,16384]{1,0:T(1,128)}, u32[]{:S(2)}) copy-start(s32[1,16384]{1,0:T(1,128)} %cell_ref.1) | copy-start | bytes 196612
  34.7 1.6 %collective-permute-start.7 = (f32[512,128]{1,0:T(8,128)S(1)}, f32[512,128]{1,0:T(8,128)S(1)}, u32[]{:S(2)}, u32[]{:S(2)}) collective-permute-start(f32[512,128]{1,0:T(8,128)S(1)} %spectral_last.1.own_ref), channel_id=1, source_target_pairs={{0,1},{1,0},{2,3},{3,2},{4,5},{5,4},{6,7},{7,6},{8,9},{9,8},{10,11... | collective-permute-start | bytes 786440 | tf_op jit(solution)/shard_map/ppermute | solution.py:399

commit v3 on v2

--- a/solution.py
+++ b/solution.py
@@ -1,4 +1,5 @@
 import functools
+import math
 
 import jax
 import jax.numpy as jnp
@@ -17,12 +18,14 @@
 MZ = 128
 BF16 = jnp.bfloat16
 F32 = jnp.float32
+MOST_CHARGE = 4.0
 CHARGE_BITS = 12
 CHARGE_UNITS = 512.0
 GATHER_CHUNK = 512
 PITCH_X = 2 * MX + 1
 PITCH_Y = GY + 1
 KX_BLOCK = 16
+NEAR_GROUPS = ((0,), (1, 2))
 VMEM_LIMIT = 36 * 2**20
 STAGE_FLOPS = 2 * 3 * (1024 * 64 * 256 + 2 * 2048 * 64 * 64)
 
@@ -80,6 +83,54 @@
     return np.concatenate(packed), places
 
 
+def exchange_rounds(bunches, pencils):
+    if bunches == 8 and pencils == 2 and SPAN == 3:
+        cycles = (((0, 1, 3, 5, 7, 6, 4, 2),), ((0, 3, 2), (7, 4, 5)), ((1, 2, 5, 6, 3, 4),))
+        rounds = []
+        for round_cycles in cycles:
+            seen = [0] * bunches
+            pairs = []
+            for cycle in round_cycles:
+                for start, end in zip(cycle, cycle[1:] + cycle[:1]):
+                    pairs.append((start * 2 + seen[start], end * 2 + seen[end]))
+                    seen[start] += 1
+                    seen[end] += 1
+            pairs += [(2 * bunch, 2 * bunch + 1) for bunch in range(bunches) if not seen[bunch]]
+            rounds.append(pairs)
+        return rounds
+    return [
+        [(bunch * pencils, (bunch - distance) * pencils + 1) for bunch in range(distance, bunches)]
+        for distance in range(SPAN, 0, -1)
+    ]
+
+
+def round_offsets(rounds, bunches, pencils):
+    met = [{bunch} for bunch in range(bunches)]
+    tables = []
+    for pairs in rounds:
+        offsets = [0] * (bunches * pencils)
+        counts = [0] * (bunches * pencils)
+        for pair in pairs:
+            for here, there in (pair, pair[::-1]):
+                bunch, source = here // pencils, there // pencils
+                if abs(bunch - source) <= SPAN and source not in met[bunch]:
+                    met[bunch].add(source)
+                    offsets[here] = bunch - source
+                    counts[here] = 1
+        tables.append((offsets, counts))
+    for bunch in range(bunches):
+        assert met[bunch] == {b for b in range(bunches) if abs(b - bunch) <= SPAN}
+    return tables
+
+
+def lookup(values, index):
+    found = jnp.int32(values[0])
+    for at, value in enumerate(values):
+        if value != values[0]:
+            found = jnp.where(index == at, jnp.int32(value), found)
+    return found
+
+
 def in_hbm(array):
     return pltpu.with_memory_space_constraint(array, pltpu.HBM)
 
@@ -188,12 +239,13 @@
     width = green_ref.shape[3]
     block = KX_BLOCK
     pencil = lax.axis_index("pencil")
-    sign = 1 - 2 * pencil
+    device = lax.axis_index("bunch") * lax.axis_size("pencil") + pencil
+    chosen = [SPAN + lookup(values, device) for values, _ in offsets]
 
     def copy(at, step):
         kx = pl.ds(step * block, block)
         return pltpu.make_async_copy(
-            green_ref.at[SPAN + sign * offsets[at], :, kx], green.at[at, :, kx], arrived.at[at, step]
+            green_ref.at[chosen[at], :, kx], green.at[at, :, kx], arrived.at[at, step]
         )
 
     for step in range(MX // block):
@@ -204,7 +256,10 @@
         return table_rows(table_ref, places, name, pencil if name in ("y", "iy") else None)
 
     for at, density_ref in enumerate(densities):
-        stage_zx(density_ref[...], table("z"), table("x"), after_z, after_x, at)
+        density = density_ref[...]
+        if min(offsets[at][1]) == 0:
+            density = density * lookup(offsets[at][1], device).astype(F32)
+        stage_zx(density, table("z"), table("x"), after_z, after_x, at)
 
     def kx_block(step):
         for at in range(count):
@@ -375,27 +430,37 @@
     part, packed = deposit(cell_deposit, charge, packed)
     tables = (packed, places)
     density = part + lax.ppermute(part, "pencil", swap)
+    rounds = exchange_rounds(bunches, pencils)
+    offsets = round_offsets(rounds, bunches, pencils)
+    particles = charge.shape[1] * pencils
+    scale = 2.0 ** (15 - math.ceil(math.log2(particles * MOST_CHARGE)))
+    sent = (density * scale).astype(jnp.float16)
     near = []
-    for distance in range(SPAN, 0, -1):
-        route = []
-        for bunch in range(distance, bunches):
-            ends = (bunch * pencils, (bunch - distance) * pencils + 1)
-            route.extend([ends, ends[::-1]])
-        near.append(lax.ppermute(density, ("bunch", "pencil"), route))
-    steps = tuple(range(SPAN, 0, -1))
-    back_steps = tuple(-step for step in steps)
+    for pairs in rounds:
+        route = [*pairs, *(pair[::-1] for pair in pairs)]
+        near.append(lax.ppermute(sent, ("bunch", "pencil"), route))
+
+    def received(array):
+        return array.astype(F32) * (1.0 / scale)
 
     def terms(offsets, densities, before, last):
         return spectral(offsets, densities, green_spectra, tables, before, last)
 
-    total = terms((0,), [density], None, False)
-    total, near[0] = lax.optimization_barrier((total, near[0]))
-    far = [lax.ppermute(each, "pencil", swap) for each in near[:-1]]
-    total = terms(steps[:-1], near[:-1], total, False)
-    total, near[-1] = lax.optimization_barrier((total, near[-1]))
-    far.append(lax.ppermute(near[-1], "pencil", swap))
-    total = terms(steps[-1:], near[-1:], total, False)
-    own = terms(back_steps, far, total, True)
+    devices = bunches * pencils
+    total = terms([([0] * devices, [1] * devices)], [density], None, False)
+    far = []
+    for group in NEAR_GROUPS:
+        arrivals = [near[at] for at in group]
+        total, arrivals = lax.optimization_barrier((total, arrivals))
+        far += [lax.ppermute(each, "pencil", swap) for each in arrivals]
+        arrivals = [received(each) for each in arrivals]
+        total = terms([offsets[at] for at in group], arrivals, total, False)
+
+    def beside(values):
+        return [values[bunch * pencils + (core + 1) % pencils] for bunch in range(bunches) for core in range(pencils)]
+
+    far_offsets = [tuple(map(beside, offsets[at])) for group in NEAR_GROUPS for at in group]
+    own = terms(far_offsets, [received(each) for each in far], total, True)
     other = lax.ppermute(own, "pencil", swap)
     return gather(own, other, cell_gather)
 

time: 45.6 us -> 39.1 us (0.86); the launches traced: 44.9 us -> 38.9 us
  starting transfers between devices: 13.4 us -> 6.46 us
  waiting for transfers between devices: 2.7 us -> 3.8 us
    ppermute x6, starting transfers between devices: 12.6 us -> 5.59 us  [the longest x3 2.95 us: per_device(): far += [lax.ppermute(each, 'pencil', swap) for each in arrivals]]
    ppermute x6, waiting for transfers between devices: 0.02 us -> 1.17 us  [the longest x3 1.16 us: per_device(): near.append(lax.ppermute(sent, ('bunch', 'pencil'), route))]
  transfers between devices with their start and end apart: 8 -> 8, of which waited for: 2 -> 3; matrix products, arithmetic and copies ran while one was open for 0% -> 0% of each run, Pallas kernels for 19% -> 22%
where the time goes in v3:
time: 39.1 us; the launch traced here: 38.9 us
  Pallas kernels  27.3 us (70%)
  starting transfers between devices  6.46 us (17%)
  waiting for transfers between devices  3.8 us (10%)
  other arithmetic  1.17 us (3%)
    pallas_call x4, Pallas kernels, spectral(): pl.pallas_call(functools.partial(spectral_kernel, places, offsets, first,...  16.4 us
    pallas_call x1, Pallas kernels, gather(): pl.pallas_call(gather_kernel, out_shape=jax.ShapeDtypeStruct((3, 1, cells...  8.57 us
    ppermute x3, starting transfers between devices, per_device(): far += [lax.ppermute(each, 'pencil', swap) for each in arrivals]  2.95 us
    ppermute x3, starting transfers between devices, per_device(): near.append(lax.ppermute(sent, ('bunch', 'pencil'), route))  2.63 us
    pallas_call x1, Pallas kernels, deposit(): pl.pallas_call(deposit_kernel, in_specs=[pl.BlockSpec(memory_space=pltpu....  2.38 us
    ppermute x1, waiting for transfers between devices, per_device(): other = lax.ppermute(own, 'pencil', swap)  1.47 us
    ppermute x3, waiting for transfers between devices, per_device(): near.append(lax.ppermute(sent, ('bunch', 'pencil'), route))  1.16 us
    ppermute x1, waiting for transfers between devices, per_device(): density = part + lax.ppermute(part, 'pencil', swap)  1.16 us
  transfers between devices with their start and end apart: 8, of which 3 were waited for; matrix products, arithmetic and copies ran while one was open for 0% of the time, Pallas kernels for 22%

profile of v3, /device:TPU:17, one launch (start us, length us, event | category | flops | bytes accessed | tf_op | source)
XLA Modules:
  0.0 38.9 jit_solution(13249238251381979289)
XLA Ops:
  0.0 1.0 %convert_add_fusion.particles_ref = s32[1,16384]{1,0:T(1,128)S(1)} fusion(bf16[1,16384]{1,0:T(2,128)(2,1)} %param.5, s32[1,16384]{1,0:T(1,128)} %param.6), kind=kLoop, calls=%fused_computation.7 | loop fusion | flops 81920 | bytes 163840 | tf_op jit(solution)/shard_map/add | solution.py:180
  1.0 2.4 %deposit.1 = (f32[256,256]{1,0:T(8,128)S(1)}, bf16[896,256]{1,0:T(8,128)(2,1)S(1)}) custom-call(s32[1,16384]{1,0:T(1,128)S(1)} %convert_add_fusion.particles_ref, bf16[896,256]{1,0:T(8,128)(2,1)} %constant.10.clone.table_hbm), custom_call_target="tpu_custom_call" | custom-call | tf_op jit(solution)/shard_map/deposit/pallas_call | solution.py:181
  3.4 0.7 %collective-permute-start = (f32[256,256]{1,0:T(8,128)S(1)}, f32[256,256]{1,0:T(8,128)S(1)}, u32[]{:S(2)}, u32[]{:S(2)}) collective-permute-start(f32[256,256]{1,0:T(8,128)S(1)} %get-tuple-element.12), channel_id=1, source_target_pairs={{0,1},{1,0},{2,3},{3,2},{4,5},{5,4},{6,7},{7,6},{8,9},{9,8},{10,11... | collective-permute-start | bytes 786440 | tf_op jit(solution)/shard_map/ppermute | solution.py:432
  4.1 1.2 %collective-permute-done = f32[256,256]{1,0:T(8,128)S(1)} collective-permute-done((f32[256,256]{1,0:T(8,128)S(1)}, f32[256,256]{1,0:T(8,128)S(1)}, u32[]{:S(2)}, u32[]{:S(2)}) %collective-permute-start) | collective-permute-done | bytes 262176 | tf_op jit(solution)/shard_map/ppermute | solution.py:432
  5.3 0.5 %collective-permute-start.1 = (f16[256,256]{1,0:T(8,128)(2,1)S(1)}, f16[256,256]{1,0:T(8,128)(2,1)S(1)}, u32[]{:S(2)}, u32[]{:S(2)}) collective-permute-start(f16[256,256]{1,0:T(8,128)(2,1)S(1)} %get-tuple-element.19), channel_id=1, source_target_pairs={{0,2},{3,6},{7,10},{11,14},{15,12},{13,8},{9,4},{5,1},{2,0},{6,3},... | collective-permute-start | bytes 393224 | tf_op jit(solution)/shard_map/ppermute | solution.py:441
  5.8 1.3 %collective-permute-start.3 = (f16[256,256]{1,0:T(8,128)(2,1)S(1)}, f16[256,256]{1,0:T(8,128)(2,1)S(1)}, u32[]{:S(2)}, u32[]{:S(2)}) collective-permute-start(f16[256,256]{1,0:T(8,128)(2,1)S(1)} %get-tuple-element.19), channel_id=1, source_target_pairs={{0,6},{7,4},{5,1},{14,8},{9,10},{11,15},{2,3},{12,13},{6,0},{4,7},... | collective-permute-start | bytes 393224 | tf_op jit(solution)/shard_map/ppermute | solution.py:441
  7.1 0.9 %collective-permute-start.4 = (f16[256,256]{1,0:T(8,128)(2,1)S(1)}, f16[256,256]{1,0:T(8,128)(2,1)S(1)}, u32[]{:S(2)}, u32[]{:S(2)}) collective-permute-start(f16[256,256]{1,0:T(8,128)(2,1)S(1)} %get-tuple-element.19), channel_id=1, source_target_pairs={{2,4},{5,10},{11,12},{13,6},{7,8},{9,3},{0,1},{14,15},{4,2},{10,5}... | collective-permute-start | bytes 393224 | tf_op jit(solution)/shard_map/ppermute | solution.py:441
  7.9 2.3 %spectral_part.3.refs_3_ = f32[2048,256]{1,0:T(8,128)S(1)} custom-call(f32[256,256]{1,0:T(8,128)S(1)} %get-tuple-element.20.refs_0_, f32[7,2,64,32,128]{4,3,2,1,0:T(8,128)} %refs_3_.1, bf16[896,256]{1,0:T(8,128)(2,1)S(1)} %get-tuple-element.13.refs_2_.refs_3_.refs_4_), custom_call_target="tpu_custom_call" | custom-call | flops 402653184 | bytes 2097152 | tf_op jit(solution)/shard_map/spectral_part/pallas_call | solution.py:355
  10.3 0.0 collective-permute-done.1
  10.3 2.4 %spectral_part.4.refs_4_ = f32[2048,256]{1,0:T(8,128)S(1)} custom-call(f32[256,256]{1,0:T(8,128)S(1)} %convert_multiply_fusion.4.refs_0_, f32[7,2,64,32,128]{4,3,2,1,0:T(8,128)} %refs_3_.1, bf16[896,256]{1,0:T(8,128)(2,1)S(1)} %get-tuple-element.13.refs_2_.refs_3_.refs_4_, f32[2048,256]{1,0:T(8,128)S(1)} %spectral_part.3.refs_3_), custom_call_target="tpu_custom_call" | custom-call | flops 402653184 | bytes 2097152 | tf_op jit(solution)/shard_map/spectral_part/pallas_call | solution.py:355
  12.7 0.0 collective-permute-done.3
  12.7 1.2 %collective-permute-done.4 = f16[256,256]{1,0:T(8,128)(2,1)S(1)} collective-permute-done((f16[256,256]{1,0:T(8,128)(2,1)S(1)}, f16[256,256]{1,0:T(8,128)(2,1)S(1)}, u32[]{:S(2)}, u32[]{:S(2)}) %collective-permute-start.4) | collective-permute-done | bytes 131104 | tf_op jit(solution)/shard_map/ppermute | solution.py:441
  13.9 2.4 %collective-permute-start.6 = (f16[256,256]{1,0:T(8,128)(2,1)S(1)}, f16[256,256]{1,0:T(8,128)(2,1)S(1)}, u32[]{:S(2)}, u32[]{:S(2)}) collective-permute-start(f16[256,256]{1,0:T(8,128)(2,1)S(1)} %collective-permute-done.4), channel_id=1, source_target_pairs={{0,1},{1,0},{2,3},{3,2},{4,5},{5,4},{6,7},{7,6},{8,9},{9,8},{10,11... | collective-permute-start | bytes 393224 | tf_op jit(solution)/shard_map/ppermute | solution.py:455
  16.3 0.1 collective-permute-start.5
  16.4 0.5 %collective-permute-start.2 = (f16[256,256]{1,0:T(8,128)(2,1)S(1)}, f16[256,256]{1,0:T(8,128)(2,1)S(1)}, u32[]{:S(2)}, u32[]{:S(2)}) collective-permute-start(f16[256,256]{1,0:T(8,128)(2,1)S(1)} %collective-permute-done.1), channel_id=1, source_target_pairs={{0,1},{1,0},{2,3},{3,2},{4,5},{5,4},{6,7},{7,6},{8,9},{9,8},{10,11... | collective-permute-start | bytes 393224 | tf_op jit(solution)/shard_map/ppermute | solution.py:455
  16.9 3.8 %spectral_part.5.refs_5_ = f32[2048,256]{1,0:T(8,128)S(1)} custom-call(f32[256,256]{1,0:T(8,128)S(1)} %get-tuple-element.22.refs_0_, f32[256,256]{1,0:T(8,128)S(1)} %get-tuple-element.21.refs_1_, f32[7,2,64,32,128]{4,3,2,1,0:T(8,128)} %refs_3_.1, bf16[896,256]{1,0:T(8,128)(2,1)S(1)} %get-tuple-element.13.refs_2_.refs_3_.refs_4_, ...), custom_call_target="tpu_custom_call" | custom-call | flops 805306368 | bytes 4194304 | tf_op jit(solution)/shard_map/spectral_part/pallas_call | solution.py:355
  20.7 0.0 collective-permute-done.6
  20.7 0.0 collective-permute-done.5
  20.8 0.0 collective-permute-done.2
  20.8 0.0 copy-start
  20.8 7.9 %spectral_last.1.own_ref = f32[512,128]{1,0:T(8,128)S(1)} custom-call(f32[256,256]{1,0:T(8,128)S(1)} %convert_multiply_fusion.5.refs_0_, f32[256,256]{1,0:T(8,128)S(1)} %convert_multiply_fusion.3.refs_1_, f32[256,256]{1,0:T(8,128)S(1)} %convert_multiply_fusion.2.refs_2_, f32[7,2,64,32,128]{4,3,2,1,0:T(8,128)} %refs_3_.1, ...), custom_call_target="tpu_custom_call" | custom-call | flops 1207959552 | bytes 6291456 | tf_op jit(solution)/shard_map/spectral_last/pallas_call | solution.py:355
  28.7 0.1 collective-permute-start.7
  28.9 1.5 %collective-permute-done.7.other_ref = f32[512,128]{1,0:T(8,128)S(1)} collective-permute-done((f32[512,128]{1,0:T(8,128)S(1)}, f32[512,128]{1,0:T(8,128)S(1)}, u32[]{:S(2)}, u32[]{:S(2)}) %collective-permute-start.7) | collective-permute-done | bytes 262176 | tf_op jit(solution)/shard_map/ppermute | solution.py:464
  30.3 0.0 copy-done
  30.3 8.6 %gather.1 = f32[3,1,16384]{2,1,0:T(1,128)} custom-call(f32[512,128]{1,0:T(8,128)S(1)} %spectral_last.1.own_ref, f32[512,128]{1,0:T(8,128)S(1)} %collective-permute-done.7.other_ref, s32[1,16384]{1,0:T(1,128)S(1)} %copy-done), custom_call_target="tpu_custom_call" | custom-call | tf_op jit(solution)/shard_map/gather/pallas_call | solution.py:416
  (6 shorter events, 0.2 us)
Async XLA Ops:
  3.4 1.9 %collective-permute-start = (f32[256,256]{1,0:T(8,128)S(1)}, f32[256,256]{1,0:T(8,128)S(1)}, u32[]{:S(2)}, u32[]{:S(2)}) collective-permute-start(f32[256,256]{1,0:T(8,128)S(1)} %get-tuple-element.12), channel_id=1, source_target_pairs={{0,1},{1,0},{2,3},{3,2},{4,5},{5,4},{6,7},{7,6},{8,9},{9,8},{10,11... | collective-permute-start | bytes 786440 | tf_op jit(solution)/shard_map/ppermute | solution.py:432
  5.3 5.0 %collective-permute-start.1 = (f16[256,256]{1,0:T(8,128)(2,1)S(1)}, f16[256,256]{1,0:T(8,128)(2,1)S(1)}, u32[]{:S(2)}, u32[]{:S(2)}) collective-permute-start(f16[256,256]{1,0:T(8,128)(2,1)S(1)} %get-tuple-element.19), channel_id=1, source_target_pairs={{0,2},{3,6},{7,10},{11,14},{15,12},{13,8},{9,4},{5,1},{2,0},{6,3},... | collective-permute-start | bytes 393224 | tf_op jit(solution)/shard_map/ppermute | solution.py:441
  5.8 6.9 %collective-permute-start.3 = (f16[256,256]{1,0:T(8,128)(2,1)S(1)}, f16[256,256]{1,0:T(8,128)(2,1)S(1)}, u32[]{:S(2)}, u32[]{:S(2)}) collective-permute-start(f16[256,256]{1,0:T(8,128)(2,1)S(1)} %get-tuple-element.19), channel_id=1, source_target_pairs={{0,6},{7,4},{5,1},{14,8},{9,10},{11,15},{2,3},{12,13},{6,0},{4,7},... | collective-permute-start | bytes 393224 | tf_op jit(solution)/shard_map/ppermute | solution.py:441
  7.1 6.8 %collective-permute-start.4 = (f16[256,256]{1,0:T(8,128)(2,1)S(1)}, f16[256,256]{1,0:T(8,128)(2,1)S(1)}, u32[]{:S(2)}, u32[]{:S(2)}) collective-permute-start(f16[256,256]{1,0:T(8,128)(2,1)S(1)} %get-tuple-element.19), channel_id=1, source_target_pairs={{2,4},{5,10},{11,12},{13,6},{7,8},{9,3},{0,1},{14,15},{4,2},{10,5}... | collective-permute-start | bytes 393224 | tf_op jit(solution)/shard_map/ppermute | solution.py:441
  13.9 6.8 %collective-permute-start.6 = (f16[256,256]{1,0:T(8,128)(2,1)S(1)}, f16[256,256]{1,0:T(8,128)(2,1)S(1)}, u32[]{:S(2)}, u32[]{:S(2)}) collective-permute-start(f16[256,256]{1,0:T(8,128)(2,1)S(1)} %collective-permute-done.4), channel_id=1, source_target_pairs={{0,1},{1,0},{2,3},{3,2},{4,5},{5,4},{6,7},{7,6},{8,9},{9,8},{10,11... | collective-permute-start | bytes 393224 | tf_op jit(solution)/shard_map/ppermute | solution.py:455
  16.3 4.4 %collective-permute-start.5 = (f16[256,256]{1,0:T(8,128)(2,1)S(1)}, f16[256,256]{1,0:T(8,128)(2,1)S(1)}, u32[]{:S(2)}, u32[]{:S(2)}) collective-permute-start(f16[256,256]{1,0:T(8,128)(2,1)S(1)} %collective-permute-done.3), channel_id=1, source_target_pairs={{0,1},{1,0},{2,3},{3,2},{4,5},{5,4},{6,7},{7,6},{8,9},{9,8},{10,11... | collective-permute-start | bytes 393224 | tf_op jit(solution)/shard_map/ppermute | solution.py:455
  16.4 4.4 %collective-permute-start.2 = (f16[256,256]{1,0:T(8,128)(2,1)S(1)}, f16[256,256]{1,0:T(8,128)(2,1)S(1)}, u32[]{:S(2)}, u32[]{:S(2)}) collective-permute-start(f16[256,256]{1,0:T(8,128)(2,1)S(1)} %collective-permute-done.1), channel_id=1, source_target_pairs={{0,1},{1,0},{2,3},{3,2},{4,5},{5,4},{6,7},{7,6},{8,9},{9,8},{10,11... | collective-permute-start | bytes 393224 | tf_op jit(solution)/shard_map/ppermute | solution.py:455
  20.8 9.5 %copy-start = (s32[1,16384]{1,0:T(1,128)S(1)}, s32[1,16384]{1,0:T(1,128)}, u32[]{:S(2)}) copy-start(s32[1,16384]{1,0:T(1,128)} %cell_ref.1) | copy-start | bytes 196612
  28.7 1.6 %collective-permute-start.7 = (f32[512,128]{1,0:T(8,128)S(1)}, f32[512,128]{1,0:T(8,128)S(1)}, u32[]{:S(2)}, u32[]{:S(2)}) collective-permute-start(f32[512,128]{1,0:T(8,128)S(1)} %spectral_last.1.own_ref), channel_id=1, source_target_pairs={{0,1},{1,0},{2,3},{3,2},{4,5},{5,4},{6,7},{7,6},{8,9},{9,8},{10,11... | collective-permute-start | bytes 786440 | tf_op jit(solution)/shard_map/ppermute | solution.py:464

commit v4 on v3

--- a/solution.py
+++ b/solution.py
@@ -24,7 +24,7 @@
 GATHER_CHUNK = 512
 PITCH_X = 2 * MX + 1
 PITCH_Y = GY + 1
-KX_BLOCK = 16
+KX_BLOCK = 32
 NEAR_GROUPS = ((0,), (1, 2))
 VMEM_LIMIT = 36 * 2**20
 STAGE_FLOPS = 2 * 3 * (1024 * 64 * 256 + 2 * 2048 * 64 * 64)
@@ -39,6 +39,11 @@
 def stacked_terms(table):
     top, rest = hi_lo(table)
     return np.concatenate([top, top, rest], axis=-1)
+
+
+def stacked_rows(table):
+    top, rest = hi_lo(table)
+    return np.block([[top, top], [rest, np.zeros_like(rest)]])
 
 
 def phases(rows, columns, period):
@@ -58,7 +63,7 @@
     for pencil in range(pencils):
         own = np.arange(pencil * width, (pencil + 1) * width)
         cos_y, sin_y = phases(own, np.arange(GY), MY)
-        forward_y.append(stacked_terms(np.block([[cos_y, sin_y], [-sin_y, cos_y]])))
+        forward_y.append(stacked_rows(np.block([[cos_y, sin_y], [-sin_y, cos_y]])))
         inverse_y.append(stacked_terms(np.concatenate([cos_y.T, sin_y.T], axis=0)))
     cos_b, sin_b = phases(np.arange(MZ), np.arange(GZ), MZ)
     inverse_z = np.block([[cos_b, sin_b], [-sin_b, cos_b]])
@@ -158,6 +163,12 @@
     return jnp.where(place == index.astype(jnp.int16), value, jnp.zeros((), BF16))
 
 
+def two_term_dot(table, value):
+    out = dot(table, jnp.concatenate(split(value), axis=0))
+    half = out.shape[0] // 2
+    return out[:half] + out[half:]
+
+
 def deposit_kernel(particles_ref, table_hbm, out_ref, table_ref, arrived):
     copy = pltpu.make_async_copy(table_hbm, table_ref, arrived)
     copy.start()
@@ -280,7 +291,7 @@
                     real = after_x[at, pl.ds(kx, GY, stride=PITCH_X), :]
                     imag = after_x[at, pl.ds(MX + kx, GY, stride=PITCH_X), :]
                     sides.append(jnp.concatenate([real, imag], axis=0))
-                out = dot(table("y"), data_terms(jnp.concatenate(sides, axis=1)))
+                out = two_term_dot(table("y"), jnp.concatenate(sides, axis=1))
                 for side in range(2):
                     kx = step * block + 2 * pair + side
                     real = out[:width, side * MZ : (side + 1) * MZ]

time: 39.1 us -> 37.9 us (0.969)
  Pallas kernels: 27.3 us -> 25.9 us
    pallas_call x4, Pallas kernels: 16.4 us -> 15 us  [spectral(): pl.pallas_call(functools.partial(spectral_kernel, places, offsets, first,...]
where the time goes in v4:
time: 37.9 us; the launch traced here: 37.7 us
  Pallas kernels  25.9 us (68%)
  starting transfers between devices  6.47 us (17%)
  waiting for transfers between devices  4.01 us (11%)
  other arithmetic  1.17 us (3%)
    pallas_call x4, Pallas kernels, spectral(): pl.pallas_call(functools.partial(spectral_kernel, places, offsets, first,...  15 us
    pallas_call x1, Pallas kernels, gather(): pl.pallas_call(gather_kernel, out_shape=jax.ShapeDtypeStruct((3, 1, cells...  8.57 us
    ppermute x3, starting transfers between devices, per_device(): far += [lax.ppermute(each, 'pencil', swap) for each in arrivals]  2.95 us
    ppermute x3, starting transfers between devices, per_device(): near.append(lax.ppermute(sent, ('bunch', 'pencil'), route))  2.63 us
    pallas_call x1, Pallas kernels, deposit(): pl.pallas_call(deposit_kernel, in_specs=[pl.BlockSpec(memory_space=pltpu....  2.38 us
    ppermute x1, waiting for transfers between devices, per_device(): other = lax.ppermute(own, 'pencil', swap)  1.45 us
    ppermute x3, waiting for transfers between devices, per_device(): near.append(lax.ppermute(sent, ('bunch', 'pencil'), route))  1.39 us
    ppermute x1, waiting for transfers between devices, per_device(): density = part + lax.ppermute(part, 'pencil', swap)  1.16 us
  transfers between devices with their start and end apart: 8, of which 3 were waited for; matrix products, arithmetic and copies ran while one was open for 0% of the time, Pallas kernels for 22%

profile of v4, /device:TPU:17, one launch (start us, length us, event | category | flops | bytes accessed | tf_op | source)
XLA Modules:
  0.0 37.7 jit_solution(9619452767524454772)
XLA Ops:
  0.0 1.0 %convert_add_fusion.particles_ref = s32[1,16384]{1,0:T(1,128)S(1)} fusion(bf16[1,16384]{1,0:T(2,128)(2,1)} %param.5, s32[1,16384]{1,0:T(1,128)} %param.6), kind=kLoop, calls=%fused_computation.7 | loop fusion | flops 81920 | bytes 163840 | tf_op jit(solution)/shard_map/add | solution.py:191
  1.0 2.4 %deposit.1 = (f32[256,256]{1,0:T(8,128)S(1)}, bf16[1024,256]{1,0:T(8,128)(2,1)S(1)}) custom-call(s32[1,16384]{1,0:T(1,128)S(1)} %convert_add_fusion.particles_ref, bf16[1024,256]{1,0:T(8,128)(2,1)} %constant.10.clone.table_hbm), custom_call_target="tpu_custom_call" | custom-call | tf_op jit(solution)/shard_map/deposit/pallas_call | solution.py:192
  3.4 0.7 %collective-permute-start = (f32[256,256]{1,0:T(8,128)S(1)}, f32[256,256]{1,0:T(8,128)S(1)}, u32[]{:S(2)}, u32[]{:S(2)}) collective-permute-start(f32[256,256]{1,0:T(8,128)S(1)} %get-tuple-element.12), channel_id=1, source_target_pairs={{0,1},{1,0},{2,3},{3,2},{4,5},{5,4},{6,7},{7,6},{8,9},{9,8},{10,11... | collective-permute-start | bytes 786440 | tf_op jit(solution)/shard_map/ppermute | solution.py:443
  4.1 1.2 %collective-permute-done = f32[256,256]{1,0:T(8,128)S(1)} collective-permute-done((f32[256,256]{1,0:T(8,128)S(1)}, f32[256,256]{1,0:T(8,128)S(1)}, u32[]{:S(2)}, u32[]{:S(2)}) %collective-permute-start) | collective-permute-done | bytes 262176 | tf_op jit(solution)/shard_map/ppermute | solution.py:443
  5.3 0.5 %collective-permute-start.1 = (f16[256,256]{1,0:T(8,128)(2,1)S(1)}, f16[256,256]{1,0:T(8,128)(2,1)S(1)}, u32[]{:S(2)}, u32[]{:S(2)}) collective-permute-start(f16[256,256]{1,0:T(8,128)(2,1)S(1)} %get-tuple-element.19), channel_id=1, source_target_pairs={{0,2},{3,6},{7,10},{11,14},{15,12},{13,8},{9,4},{5,1},{2,0},{6,3},... | collective-permute-start | bytes 393224 | tf_op jit(solution)/shard_map/ppermute | solution.py:452
  5.8 1.3 %collective-permute-start.3 = (f16[256,256]{1,0:T(8,128)(2,1)S(1)}, f16[256,256]{1,0:T(8,128)(2,1)S(1)}, u32[]{:S(2)}, u32[]{:S(2)}) collective-permute-start(f16[256,256]{1,0:T(8,128)(2,1)S(1)} %get-tuple-element.19), channel_id=1, source_target_pairs={{0,6},{7,4},{5,1},{14,8},{9,10},{11,15},{2,3},{12,13},{6,0},{4,7},... | collective-permute-start | bytes 393224 | tf_op jit(solution)/shard_map/ppermute | solution.py:452
  7.1 0.9 %collective-permute-start.4 = (f16[256,256]{1,0:T(8,128)(2,1)S(1)}, f16[256,256]{1,0:T(8,128)(2,1)S(1)}, u32[]{:S(2)}, u32[]{:S(2)}) collective-permute-start(f16[256,256]{1,0:T(8,128)(2,1)S(1)} %get-tuple-element.19), channel_id=1, source_target_pairs={{2,4},{5,10},{11,12},{13,6},{7,8},{9,3},{0,1},{14,15},{4,2},{10,5}... | collective-permute-start | bytes 393224 | tf_op jit(solution)/shard_map/ppermute | solution.py:452
  7.9 2.1 %spectral_part.3.refs_3_ = f32[2048,256]{1,0:T(8,128)S(1)} custom-call(f32[256,256]{1,0:T(8,128)S(1)} %get-tuple-element.20.refs_0_, f32[7,2,64,32,128]{4,3,2,1,0:T(8,128)} %refs_3_.1, bf16[1024,256]{1,0:T(8,128)(2,1)S(1)} %get-tuple-element.13.refs_2_.refs_3_.refs_4_), custom_call_target="tpu_custom_call" | custom-call | flops 402653184 | bytes 2097152 | tf_op jit(solution)/shard_map/spectral_part/pallas_call | solution.py:366
  10.1 0.0 collective-permute-done.1
  10.1 2.3 %spectral_part.4.refs_4_ = f32[2048,256]{1,0:T(8,128)S(1)} custom-call(f32[256,256]{1,0:T(8,128)S(1)} %convert_multiply_fusion.4.refs_0_, f32[7,2,64,32,128]{4,3,2,1,0:T(8,128)} %refs_3_.1, bf16[1024,256]{1,0:T(8,128)(2,1)S(1)} %get-tuple-element.13.refs_2_.refs_3_.refs_4_, f32[2048,256]{1,0:T(8,128)S(1)} %spectral_part.3.refs_3_), custom_call_target="tpu_custom_call" | custom-call | flops 402653184 | bytes 2097152 | tf_op jit(solution)/shard_map/spectral_part/pallas_call | solution.py:366
  12.5 0.0 collective-permute-done.3
  12.5 1.4 %collective-permute-done.4 = f16[256,256]{1,0:T(8,128)(2,1)S(1)} collective-permute-done((f16[256,256]{1,0:T(8,128)(2,1)S(1)}, f16[256,256]{1,0:T(8,128)(2,1)S(1)}, u32[]{:S(2)}, u32[]{:S(2)}) %collective-permute-start.4) | collective-permute-done | bytes 131104 | tf_op jit(solution)/shard_map/ppermute | solution.py:452
  13.9 2.4 %collective-permute-start.6 = (f16[256,256]{1,0:T(8,128)(2,1)S(1)}, f16[256,256]{1,0:T(8,128)(2,1)S(1)}, u32[]{:S(2)}, u32[]{:S(2)}) collective-permute-start(f16[256,256]{1,0:T(8,128)(2,1)S(1)} %collective-permute-done.4), channel_id=1, source_target_pairs={{0,1},{1,0},{2,3},{3,2},{4,5},{5,4},{6,7},{7,6},{8,9},{9,8},{10,11... | collective-permute-start | bytes 393224 | tf_op jit(solution)/shard_map/ppermute | solution.py:466
  16.3 0.1 collective-permute-start.5
  16.4 0.5 %collective-permute-start.2 = (f16[256,256]{1,0:T(8,128)(2,1)S(1)}, f16[256,256]{1,0:T(8,128)(2,1)S(1)}, u32[]{:S(2)}, u32[]{:S(2)}) collective-permute-start(f16[256,256]{1,0:T(8,128)(2,1)S(1)} %collective-permute-done.1), channel_id=1, source_target_pairs={{0,1},{1,0},{2,3},{3,2},{4,5},{5,4},{6,7},{7,6},{8,9},{9,8},{10,11... | collective-permute-start | bytes 393224 | tf_op jit(solution)/shard_map/ppermute | solution.py:466
  16.9 3.7 %spectral_part.5.refs_5_ = f32[2048,256]{1,0:T(8,128)S(1)} custom-call(f32[256,256]{1,0:T(8,128)S(1)} %get-tuple-element.22.refs_0_, f32[256,256]{1,0:T(8,128)S(1)} %get-tuple-element.21.refs_1_, f32[7,2,64,32,128]{4,3,2,1,0:T(8,128)} %refs_3_.1, bf16[1024,256]{1,0:T(8,128)(2,1)S(1)} %get-tuple-element.13.refs_2_.refs_3_.refs_4_, ...), custom_call_target="tpu_custom_call" | custom-call | flops 805306368 | bytes 4194304 | tf_op jit(solution)/shard_map/spectral_part/pallas_call | solution.py:366
  20.6 0.0 collective-permute-done.6
  20.7 0.0 collective-permute-done.5
  20.7 0.0 collective-permute-done.2
  20.8 0.0 copy-start
  20.8 6.8 %spectral_last.1.own_ref = f32[512,128]{1,0:T(8,128)S(1)} custom-call(f32[256,256]{1,0:T(8,128)S(1)} %convert_multiply_fusion.5.refs_0_, f32[256,256]{1,0:T(8,128)S(1)} %convert_multiply_fusion.3.refs_1_, f32[256,256]{1,0:T(8,128)S(1)} %convert_multiply_fusion.2.refs_2_, f32[7,2,64,32,128]{4,3,2,1,0:T(8,128)} %refs_3_.1, ...), custom_call_target="tpu_custom_call" | custom-call | flops 1207959552 | bytes 6291456 | tf_op jit(solution)/shard_map/spectral_last/pallas_call | solution.py:366
  27.5 0.1 collective-permute-start.7
  27.7 1.5 %collective-permute-done.7.other_ref = f32[512,128]{1,0:T(8,128)S(1)} collective-permute-done((f32[512,128]{1,0:T(8,128)S(1)}, f32[512,128]{1,0:T(8,128)S(1)}, u32[]{:S(2)}, u32[]{:S(2)}) %collective-permute-start.7) | collective-permute-done | bytes 262176 | tf_op jit(solution)/shard_map/ppermute | solution.py:475
  29.1 0.0 copy-done
  29.1 8.6 %gather.1 = f32[3,1,16384]{2,1,0:T(1,128)} custom-call(f32[512,128]{1,0:T(8,128)S(1)} %spectral_last.1.own_ref, f32[512,128]{1,0:T(8,128)S(1)} %collective-permute-done.7.other_ref, s32[1,16384]{1,0:T(1,128)S(1)} %copy-done), custom_call_target="tpu_custom_call" | custom-call | tf_op jit(solution)/shard_map/gather/pallas_call | solution.py:427
  (6 shorter events, 0.2 us)
Async XLA Ops:
  3.4 1.9 %collective-permute-start = (f32[256,256]{1,0:T(8,128)S(1)}, f32[256,256]{1,0:T(8,128)S(1)}, u32[]{:S(2)}, u32[]{:S(2)}) collective-permute-start(f32[256,256]{1,0:T(8,128)S(1)} %get-tuple-element.12), channel_id=1, source_target_pairs={{0,1},{1,0},{2,3},{3,2},{4,5},{5,4},{6,7},{7,6},{8,9},{9,8},{10,11... | collective-permute-start | bytes 786440 | tf_op jit(solution)/shard_map/ppermute | solution.py:443
  5.3 4.8 %collective-permute-start.1 = (f16[256,256]{1,0:T(8,128)(2,1)S(1)}, f16[256,256]{1,0:T(8,128)(2,1)S(1)}, u32[]{:S(2)}, u32[]{:S(2)}) collective-permute-start(f16[256,256]{1,0:T(8,128)(2,1)S(1)} %get-tuple-element.19), channel_id=1, source_target_pairs={{0,2},{3,6},{7,10},{11,14},{15,12},{13,8},{9,4},{5,1},{2,0},{6,3},... | collective-permute-start | bytes 393224 | tf_op jit(solution)/shard_map/ppermute | solution.py:452
  5.8 6.7 %collective-permute-start.3 = (f16[256,256]{1,0:T(8,128)(2,1)S(1)}, f16[256,256]{1,0:T(8,128)(2,1)S(1)}, u32[]{:S(2)}, u32[]{:S(2)}) collective-permute-start(f16[256,256]{1,0:T(8,128)(2,1)S(1)} %get-tuple-element.19), channel_id=1, source_target_pairs={{0,6},{7,4},{5,1},{14,8},{9,10},{11,15},{2,3},{12,13},{6,0},{4,7},... | collective-permute-start | bytes 393224 | tf_op jit(solution)/shard_map/ppermute | solution.py:452
  7.1 6.8 %collective-permute-start.4 = (f16[256,256]{1,0:T(8,128)(2,1)S(1)}, f16[256,256]{1,0:T(8,128)(2,1)S(1)}, u32[]{:S(2)}, u32[]{:S(2)}) collective-permute-start(f16[256,256]{1,0:T(8,128)(2,1)S(1)} %get-tuple-element.19), channel_id=1, source_target_pairs={{2,4},{5,10},{11,12},{13,6},{7,8},{9,3},{0,1},{14,15},{4,2},{10,5}... | collective-permute-start | bytes 393224 | tf_op jit(solution)/shard_map/ppermute | solution.py:452
  13.9 6.8 %collective-permute-start.6 = (f16[256,256]{1,0:T(8,128)(2,1)S(1)}, f16[256,256]{1,0:T(8,128)(2,1)S(1)}, u32[]{:S(2)}, u32[]{:S(2)}) collective-permute-start(f16[256,256]{1,0:T(8,128)(2,1)S(1)} %collective-permute-done.4), channel_id=1, source_target_pairs={{0,1},{1,0},{2,3},{3,2},{4,5},{5,4},{6,7},{7,6},{8,9},{9,8},{10,11... | collective-permute-start | bytes 393224 | tf_op jit(solution)/shard_map/ppermute | solution.py:466
  16.3 4.4 %collective-permute-start.5 = (f16[256,256]{1,0:T(8,128)(2,1)S(1)}, f16[256,256]{1,0:T(8,128)(2,1)S(1)}, u32[]{:S(2)}, u32[]{:S(2)}) collective-permute-start(f16[256,256]{1,0:T(8,128)(2,1)S(1)} %collective-permute-done.3), channel_id=1, source_target_pairs={{0,1},{1,0},{2,3},{3,2},{4,5},{5,4},{6,7},{7,6},{8,9},{9,8},{10,11... | collective-permute-start | bytes 393224 | tf_op jit(solution)/shard_map/ppermute | solution.py:466
  16.4 4.3 %collective-permute-start.2 = (f16[256,256]{1,0:T(8,128)(2,1)S(1)}, f16[256,256]{1,0:T(8,128)(2,1)S(1)}, u32[]{:S(2)}, u32[]{:S(2)}) collective-permute-start(f16[256,256]{1,0:T(8,128)(2,1)S(1)} %collective-permute-done.1), channel_id=1, source_target_pairs={{0,1},{1,0},{2,3},{3,2},{4,5},{5,4},{6,7},{7,6},{8,9},{9,8},{10,11... | collective-permute-start | bytes 393224 | tf_op jit(solution)/shard_map/ppermute | solution.py:466
  20.8 8.4 %copy-start = (s32[1,16384]{1,0:T(1,128)S(1)}, s32[1,16384]{1,0:T(1,128)}, u32[]{:S(2)}) copy-start(s32[1,16384]{1,0:T(1,128)} %cell_ref.1) | copy-start | bytes 196612
  27.5 1.6 %collective-permute-start.7 = (f32[512,128]{1,0:T(8,128)S(1)}, f32[512,128]{1,0:T(8,128)S(1)}, u32[]{:S(2)}, u32[]{:S(2)}) collective-permute-start(f32[512,128]{1,0:T(8,128)S(1)} %spectral_last.1.own_ref), channel_id=1, source_target_pairs={{0,1},{1,0},{2,3},{3,2},{4,5},{5,4},{6,7},{7,6},{8,9},{9,8},{10,11... | collective-permute-start | bytes 786440 | tf_op jit(solution)/shard_map/ppermute | solution.py:475

commit v5 on v4

--- a/solution.py
+++ b/solution.py
@@ -440,19 +440,20 @@
     packed, places = tables
     part, packed = deposit(cell_deposit, charge, packed)
     tables = (packed, places)
-    density = part + lax.ppermute(part, "pencil", swap)
+    particles = charge.shape[1] * pencils
+    scale = 2.0 ** (15 - math.ceil(math.log2(particles * MOST_CHARGE)))
+    def received(array):
+        return array.astype(F32) * (1.0 / scale)
+
+    partial = (part * scale).astype(jnp.float16)
+    density = part + received(lax.ppermute(partial, "pencil", swap))
     rounds = exchange_rounds(bunches, pencils)
     offsets = round_offsets(rounds, bunches, pencils)
-    particles = charge.shape[1] * pencils
-    scale = 2.0 ** (15 - math.ceil(math.log2(particles * MOST_CHARGE)))
     sent = (density * scale).astype(jnp.float16)
     near = []
     for pairs in rounds:
         route = [*pairs, *(pair[::-1] for pair in pairs)]
         near.append(lax.ppermute(sent, ("bunch", "pencil"), route))
-
-    def received(array):
-        return array.astype(F32) * (1.0 / scale)
 
     def terms(offsets, densities, before, last):
         return spectral(offsets, densities, green_spectra, tables, before, last)

time: 37.9 us -> 37.8 us (level)
  no operation moved by 1% of the time
where the time goes in v5:
time: 37.8 us; the launch traced here: 37.6 us
  Pallas kernels  25.9 us (69%)
  starting transfers between devices  6.41 us (17%)
  waiting for transfers between devices  3.91 us (10%)
  other arithmetic  1.21 us (3%)
    pallas_call x4, Pallas kernels, spectral(): pl.pallas_call(functools.partial(spectral_kernel, places, offsets, first,...  15 us
    pallas_call x1, Pallas kernels, gather(): pl.pallas_call(gather_kernel, out_shape=jax.ShapeDtypeStruct((3, 1, cells...  8.57 us
    ppermute x3, starting transfers between devices, per_device(): far += [lax.ppermute(each, 'pencil', swap) for each in arrivals]  2.93 us
    ppermute x3, starting transfers between devices, per_device(): near.append(lax.ppermute(sent, ('bunch', 'pencil'), route))  2.62 us
    pallas_call x1, Pallas kernels, deposit(): pl.pallas_call(deposit_kernel, in_specs=[pl.BlockSpec(memory_space=pltpu....  2.38 us
    ppermute x1, waiting for transfers between devices, per_device(): other = lax.ppermute(own, 'pencil', swap)  1.49 us
    ppermute x3, waiting for transfers between devices, per_device(): near.append(lax.ppermute(sent, ('bunch', 'pencil'), route))  1.43 us
    ppermute x1, waiting for transfers between devices, per_device(): density = part + received(lax.ppermute(partial, 'pencil', swap))  0.99 us
  transfers between devices with their start and end apart: 8, of which 3 were waited for; matrix products, arithmetic and copies ran while one was open for 0% of the time, Pallas kernels for 22%

profile of v5, /device:TPU:17, one launch (start us, length us, event | category | flops | bytes accessed | tf_op | source)
XLA Modules:
  0.0 37.6 jit_solution(4681962851448533731)
XLA Ops:
  0.0 1.0 %convert_add_fusion.particles_ref = s32[1,16384]{1,0:T(1,128)S(1)} fusion(bf16[1,16384]{1,0:T(2,128)(2,1)} %param.5, s32[1,16384]{1,0:T(1,128)} %param.6), kind=kLoop, calls=%fused_computation.9 | loop fusion | flops 81920 | bytes 163840 | tf_op jit(solution)/shard_map/add | solution.py:191
  1.0 2.4 %deposit.1 = (f32[256,256]{1,0:T(8,128)S(1)}, bf16[1024,256]{1,0:T(8,128)(2,1)S(1)}) custom-call(s32[1,16384]{1,0:T(1,128)S(1)} %convert_add_fusion.particles_ref, bf16[1024,256]{1,0:T(8,128)(2,1)} %constant.10.clone.table_hbm), custom_call_target="tpu_custom_call" | custom-call | tf_op jit(solution)/shard_map/deposit/pallas_call | solution.py:192
  3.4 0.7 %collective-permute-start = (f16[256,256]{1,0:T(8,128)(2,1)S(1)}, f16[256,256]{1,0:T(8,128)(2,1)S(1)}, u32[]{:S(2)}, u32[]{:S(2)}) collective-permute-start(f16[256,256]{1,0:T(8,128)(2,1)S(1)} %multiply_convert_fusion.1), channel_id=1, source_target_pairs={{0,1},{1,0},{2,3},{3,2},{4,5},{5,4},{6,7},{7,6},{8,9},{9,8},{10,11... | collective-permute-start | bytes 393224 | tf_op jit(solution)/shard_map/ppermute | solution.py:449
  4.1 1.0 %collective-permute-done = f16[256,256]{1,0:T(8,128)(2,1)S(1)} collective-permute-done((f16[256,256]{1,0:T(8,128)(2,1)S(1)}, f16[256,256]{1,0:T(8,128)(2,1)S(1)}, u32[]{:S(2)}, u32[]{:S(2)}) %collective-permute-start) | collective-permute-done | bytes 131104 | tf_op jit(solution)/shard_map/ppermute | solution.py:449
  5.1 0.1 multiply_convert_fusion
  5.2 0.5 %collective-permute-start.1 = (f16[256,256]{1,0:T(8,128)(2,1)S(1)}, f16[256,256]{1,0:T(8,128)(2,1)S(1)}, u32[]{:S(2)}, u32[]{:S(2)}) collective-permute-start(f16[256,256]{1,0:T(8,128)(2,1)S(1)} %get-tuple-element.19), channel_id=1, source_target_pairs={{0,2},{3,6},{7,10},{11,14},{15,12},{13,8},{9,4},{5,1},{2,0},{6,3},... | collective-permute-start | bytes 393224 | tf_op jit(solution)/shard_map/ppermute | solution.py:456
  5.7 1.3 %collective-permute-start.3 = (f16[256,256]{1,0:T(8,128)(2,1)S(1)}, f16[256,256]{1,0:T(8,128)(2,1)S(1)}, u32[]{:S(2)}, u32[]{:S(2)}) collective-permute-start(f16[256,256]{1,0:T(8,128)(2,1)S(1)} %get-tuple-element.19), channel_id=1, source_target_pairs={{0,6},{7,4},{5,1},{14,8},{9,10},{11,15},{2,3},{12,13},{6,0},{4,7},... | collective-permute-start | bytes 393224 | tf_op jit(solution)/shard_map/ppermute | solution.py:456
  6.9 0.9 %collective-permute-start.4 = (f16[256,256]{1,0:T(8,128)(2,1)S(1)}, f16[256,256]{1,0:T(8,128)(2,1)S(1)}, u32[]{:S(2)}, u32[]{:S(2)}) collective-permute-start(f16[256,256]{1,0:T(8,128)(2,1)S(1)} %get-tuple-element.19), channel_id=1, source_target_pairs={{2,4},{5,10},{11,12},{13,6},{7,8},{9,3},{0,1},{14,15},{4,2},{10,5}... | collective-permute-start | bytes 393224 | tf_op jit(solution)/shard_map/ppermute | solution.py:456
  7.8 2.1 %spectral_part.3.refs_3_ = f32[2048,256]{1,0:T(8,128)S(1)} custom-call(f32[256,256]{1,0:T(8,128)S(1)} %get-tuple-element.20.refs_0_, f32[7,2,64,32,128]{4,3,2,1,0:T(8,128)} %refs_3_.1, bf16[1024,256]{1,0:T(8,128)(2,1)S(1)} %get-tuple-element.13.refs_2_.refs_3_.refs_4_), custom_call_target="tpu_custom_call" | custom-call | flops 402653184 | bytes 2097152 | tf_op jit(solution)/shard_map/spectral_part/pallas_call | solution.py:366
  9.9 0.0 collective-permute-done.1
  10.0 2.3 %spectral_part.4.refs_4_ = f32[2048,256]{1,0:T(8,128)S(1)} custom-call(f32[256,256]{1,0:T(8,128)S(1)} %convert_multiply_fusion.4.refs_0_, f32[7,2,64,32,128]{4,3,2,1,0:T(8,128)} %refs_3_.1, bf16[1024,256]{1,0:T(8,128)(2,1)S(1)} %get-tuple-element.13.refs_2_.refs_3_.refs_4_, f32[2048,256]{1,0:T(8,128)S(1)} %spectral_part.3.refs_3_), custom_call_target="tpu_custom_call" | custom-call | flops 402653184 | bytes 2097152 | tf_op jit(solution)/shard_map/spectral_part/pallas_call | solution.py:366
  12.3 0.0 collective-permute-done.3
  12.3 1.4 %collective-permute-done.4 = f16[256,256]{1,0:T(8,128)(2,1)S(1)} collective-permute-done((f16[256,256]{1,0:T(8,128)(2,1)S(1)}, f16[256,256]{1,0:T(8,128)(2,1)S(1)}, u32[]{:S(2)}, u32[]{:S(2)}) %collective-permute-start.4) | collective-permute-done | bytes 131104 | tf_op jit(solution)/shard_map/ppermute | solution.py:456
  13.7 2.4 %collective-permute-start.6 = (f16[256,256]{1,0:T(8,128)(2,1)S(1)}, f16[256,256]{1,0:T(8,128)(2,1)S(1)}, u32[]{:S(2)}, u32[]{:S(2)}) collective-permute-start(f16[256,256]{1,0:T(8,128)(2,1)S(1)} %collective-permute-done.4), channel_id=1, source_target_pairs={{0,1},{1,0},{2,3},{3,2},{4,5},{5,4},{6,7},{7,6},{8,9},{9,8},{10,11... | collective-permute-start | bytes 393224 | tf_op jit(solution)/shard_map/ppermute | solution.py:467
  16.2 0.1 collective-permute-start.5
  16.2 0.5 %collective-permute-start.2 = (f16[256,256]{1,0:T(8,128)(2,1)S(1)}, f16[256,256]{1,0:T(8,128)(2,1)S(1)}, u32[]{:S(2)}, u32[]{:S(2)}) collective-permute-start(f16[256,256]{1,0:T(8,128)(2,1)S(1)} %collective-permute-done.1), channel_id=1, source_target_pairs={{0,1},{1,0},{2,3},{3,2},{4,5},{5,4},{6,7},{7,6},{8,9},{9,8},{10,11... | collective-permute-start | bytes 393224 | tf_op jit(solution)/shard_map/ppermute | solution.py:467
  16.7 3.8 %spectral_part.5.refs_5_ = f32[2048,256]{1,0:T(8,128)S(1)} custom-call(f32[256,256]{1,0:T(8,128)S(1)} %get-tuple-element.22.refs_0_, f32[256,256]{1,0:T(8,128)S(1)} %get-tuple-element.21.refs_1_, f32[7,2,64,32,128]{4,3,2,1,0:T(8,128)} %refs_3_.1, bf16[1024,256]{1,0:T(8,128)(2,1)S(1)} %get-tuple-element.13.refs_2_.refs_3_.refs_4_, ...), custom_call_target="tpu_custom_call" | custom-call | flops 805306368 | bytes 4194304 | tf_op jit(solution)/shard_map/spectral_part/pallas_call | solution.py:366
  20.5 0.0 collective-permute-done.6
  20.5 0.0 collective-permute-done.5
  20.6 0.0 collective-permute-done.2
  20.6 0.0 copy-start
  20.6 6.8 %spectral_last.1.own_ref = f32[512,128]{1,0:T(8,128)S(1)} custom-call(f32[256,256]{1,0:T(8,128)S(1)} %convert_multiply_fusion.5.refs_0_, f32[256,256]{1,0:T(8,128)S(1)} %convert_multiply_fusion.3.refs_1_, f32[256,256]{1,0:T(8,128)S(1)} %convert_multiply_fusion.2.refs_2_, f32[7,2,64,32,128]{4,3,2,1,0:T(8,128)} %refs_3_.1, ...), custom_call_target="tpu_custom_call" | custom-call | flops 1207959552 | bytes 6291456 | tf_op jit(solution)/shard_map/spectral_last/pallas_call | solution.py:366
  27.4 0.1 collective-permute-start.7
  27.5 1.5 %collective-permute-done.7.other_ref = f32[512,128]{1,0:T(8,128)S(1)} collective-permute-done((f32[512,128]{1,0:T(8,128)S(1)}, f32[512,128]{1,0:T(8,128)S(1)}, u32[]{:S(2)}, u32[]{:S(2)}) %collective-permute-start.7) | collective-permute-done | bytes 262176 | tf_op jit(solution)/shard_map/ppermute | solution.py:476
  29.0 0.0 copy-done
  29.0 8.6 %gather.1 = f32[3,1,16384]{2,1,0:T(1,128)} custom-call(f32[512,128]{1,0:T(8,128)S(1)} %spectral_last.1.own_ref, f32[512,128]{1,0:T(8,128)S(1)} %collective-permute-done.7.other_ref, s32[1,16384]{1,0:T(1,128)S(1)} %copy-done), custom_call_target="tpu_custom_call" | custom-call | tf_op jit(solution)/shard_map/gather/pallas_call | solution.py:427
  (6 shorter events, 0.2 us)
Async XLA Ops:
  3.4 1.7 %collective-permute-start = (f16[256,256]{1,0:T(8,128)(2,1)S(1)}, f16[256,256]{1,0:T(8,128)(2,1)S(1)}, u32[]{:S(2)}, u32[]{:S(2)}) collective-permute-start(f16[256,256]{1,0:T(8,128)(2,1)S(1)} %multiply_convert_fusion.1), channel_id=1, source_target_pairs={{0,1},{1,0},{2,3},{3,2},{4,5},{5,4},{6,7},{7,6},{8,9},{9,8},{10,11... | collective-permute-start | bytes 393224 | tf_op jit(solution)/shard_map/ppermute | solution.py:449
  5.2 4.8 %collective-permute-start.1 = (f16[256,256]{1,0:T(8,128)(2,1)S(1)}, f16[256,256]{1,0:T(8,128)(2,1)S(1)}, u32[]{:S(2)}, u32[]{:S(2)}) collective-permute-start(f16[256,256]{1,0:T(8,128)(2,1)S(1)} %get-tuple-element.19), channel_id=1, source_target_pairs={{0,2},{3,6},{7,10},{11,14},{15,12},{13,8},{9,4},{5,1},{2,0},{6,3},... | collective-permute-start | bytes 393224 | tf_op jit(solution)/shard_map/ppermute | solution.py:456
  5.7 6.7 %collective-permute-start.3 = (f16[256,256]{1,0:T(8,128)(2,1)S(1)}, f16[256,256]{1,0:T(8,128)(2,1)S(1)}, u32[]{:S(2)}, u32[]{:S(2)}) collective-permute-start(f16[256,256]{1,0:T(8,128)(2,1)S(1)} %get-tuple-element.19), channel_id=1, source_target_pairs={{0,6},{7,4},{5,1},{14,8},{9,10},{11,15},{2,3},{12,13},{6,0},{4,7},... | collective-permute-start | bytes 393224 | tf_op jit(solution)/shard_map/ppermute | solution.py:456
  6.9 6.8 %collective-permute-start.4 = (f16[256,256]{1,0:T(8,128)(2,1)S(1)}, f16[256,256]{1,0:T(8,128)(2,1)S(1)}, u32[]{:S(2)}, u32[]{:S(2)}) collective-permute-start(f16[256,256]{1,0:T(8,128)(2,1)S(1)} %get-tuple-element.19), channel_id=1, source_target_pairs={{2,4},{5,10},{11,12},{13,6},{7,8},{9,3},{0,1},{14,15},{4,2},{10,5}... | collective-permute-start | bytes 393224 | tf_op jit(solution)/shard_map/ppermute | solution.py:456
  13.7 6.8 %collective-permute-start.6 = (f16[256,256]{1,0:T(8,128)(2,1)S(1)}, f16[256,256]{1,0:T(8,128)(2,1)S(1)}, u32[]{:S(2)}, u32[]{:S(2)}) collective-permute-start(f16[256,256]{1,0:T(8,128)(2,1)S(1)} %collective-permute-done.4), channel_id=1, source_target_pairs={{0,1},{1,0},{2,3},{3,2},{4,5},{5,4},{6,7},{7,6},{8,9},{9,8},{10,11... | collective-permute-start | bytes 393224 | tf_op jit(solution)/shard_map/ppermute | solution.py:467
  16.2 4.4 %collective-permute-start.5 = (f16[256,256]{1,0:T(8,128)(2,1)S(1)}, f16[256,256]{1,0:T(8,128)(2,1)S(1)}, u32[]{:S(2)}, u32[]{:S(2)}) collective-permute-start(f16[256,256]{1,0:T(8,128)(2,1)S(1)} %collective-permute-done.3), channel_id=1, source_target_pairs={{0,1},{1,0},{2,3},{3,2},{4,5},{5,4},{6,7},{7,6},{8,9},{9,8},{10,11... | collective-permute-start | bytes 393224 | tf_op jit(solution)/shard_map/ppermute | solution.py:467
  16.2 4.3 %collective-permute-start.2 = (f16[256,256]{1,0:T(8,128)(2,1)S(1)}, f16[256,256]{1,0:T(8,128)(2,1)S(1)}, u32[]{:S(2)}, u32[]{:S(2)}) collective-permute-start(f16[256,256]{1,0:T(8,128)(2,1)S(1)} %collective-permute-done.1), channel_id=1, source_target_pairs={{0,1},{1,0},{2,3},{3,2},{4,5},{5,4},{6,7},{7,6},{8,9},{9,8},{10,11... | collective-permute-start | bytes 393224 | tf_op jit(solution)/shard_map/ppermute | solution.py:467
  20.6 8.4 %copy-start = (s32[1,16384]{1,0:T(1,128)S(1)}, s32[1,16384]{1,0:T(1,128)}, u32[]{:S(2)}) copy-start(s32[1,16384]{1,0:T(1,128)} %cell_ref.1) | copy-start | bytes 196612
  27.4 1.6 %collective-permute-start.7 = (f32[512,128]{1,0:T(8,128)S(1)}, f32[512,128]{1,0:T(8,128)S(1)}, u32[]{:S(2)}, u32[]{:S(2)}) collective-permute-start(f32[512,128]{1,0:T(8,128)S(1)} %spectral_last.1.own_ref), channel_id=1, source_target_pairs={{0,1},{1,0},{2,3},{3,2},{4,5},{5,4},{6,7},{7,6},{8,9},{9,8},{10,11... | collective-permute-start | bytes 786440 | tf_op jit(solution)/shard_map/ppermute | solution.py:476

commit v6 on v5

--- a/solution.py
+++ b/solution.py
@@ -464,7 +464,8 @@
     for group in NEAR_GROUPS:
         arrivals = [near[at] for at in group]
         total, arrivals = lax.optimization_barrier((total, arrivals))
-        far += [lax.ppermute(each, "pencil", swap) for each in arrivals]
+        beyond = lax.ppermute(jnp.concatenate(arrivals), "pencil", swap)
+        far += jnp.split(beyond, len(group))
         arrivals = [received(each) for each in arrivals]
         total = terms([offsets[at] for at in group], arrivals, total, False)
 

time: 37.8 us -> 37.3 us (0.987)
  waiting for transfers between devices: 3.91 us -> 3.12 us
    ppermute x3, waiting for transfers between devices: 1.43 us -> 0.6 us  [per_device(): near.append(lax.ppermute(sent, ('bunch', 'pencil'), route))]
    ppermute x3 -> x2, starting transfers between devices: 2.93 us -> 3.26 us  [per_device(): beyond = lax.ppermute(jnp.concatenate(arrivals), 'pencil', swap)]
  transfers between devices with their start and end apart: 8 -> 7, of which waited for: 3 -> 3; matrix products, arithmetic and copies ran while one was open for 0% -> 0% of each run, Pallas kernels for 22% -> 22%
where the time goes in v6:
time: 37.3 us; the launch traced here: 37.1 us
  Pallas kernels  25.9 us (69%)
  starting transfers between devices  6.69 us (18%)
  waiting for transfers between devices  3.12 us (8%)
  other arithmetic  1.27 us (3%)
    pallas_call x4, Pallas kernels, spectral(): pl.pallas_call(functools.partial(spectral_kernel, places, offsets, first,...  15 us
    pallas_call x1, Pallas kernels, gather(): pl.pallas_call(gather_kernel, out_shape=jax.ShapeDtypeStruct((3, 1, cells...  8.57 us
    ppermute x2, starting transfers between devices, per_device(): beyond = lax.ppermute(jnp.concatenate(arrivals), 'pencil', swap)  3.26 us
    ppermute x3, starting transfers between devices, per_device(): near.append(lax.ppermute(sent, ('bunch', 'pencil'), route))  2.62 us
    pallas_call x1, Pallas kernels, deposit(): pl.pallas_call(deposit_kernel, in_specs=[pl.BlockSpec(memory_space=pltpu....  2.38 us
    ppermute x1, waiting for transfers between devices, per_device(): other = lax.ppermute(own, 'pencil', swap)  1.52 us
    ppermute x1, waiting for transfers between devices, per_device(): density = part + received(lax.ppermute(partial, 'pencil', swap))  0.99 us
    add x1, other arithmetic, deposit(): particles = (cells << CHARGE_BITS) + units  0.98 us
  transfers between devices with their start and end apart: 7, of which 3 were waited for; matrix products, arithmetic and copies ran while one was open for 0% of the time, Pallas kernels for 22%

profile of v6, /device:TPU:17, one launch (start us, length us, event | category | flops | bytes accessed | tf_op | source)
XLA Modules:
  0.0 37.1 jit_solution(16780582310150413050)
XLA Ops:
  0.0 1.0 %convert_add_fusion.particles_ref = s32[1,16384]{1,0:T(1,128)S(1)} fusion(bf16[1,16384]{1,0:T(2,128)(2,1)} %param.5, s32[1,16384]{1,0:T(1,128)} %param.6), kind=kLoop, calls=%fused_computation.10 | loop fusion | flops 81920 | bytes 163840 | tf_op jit(solution)/shard_map/add | solution.py:191
  1.0 2.4 %deposit.1 = (f32[256,256]{1,0:T(8,128)S(1)}, bf16[1024,256]{1,0:T(8,128)(2,1)S(1)}) custom-call(s32[1,16384]{1,0:T(1,128)S(1)} %convert_add_fusion.particles_ref, bf16[1024,256]{1,0:T(8,128)(2,1)} %constant.10.clone.table_hbm), custom_call_target="tpu_custom_call" | custom-call | tf_op jit(solution)/shard_map/deposit/pallas_call | solution.py:192
  3.4 0.7 %collective-permute-start = (f16[256,256]{1,0:T(8,128)(2,1)S(1)}, f16[256,256]{1,0:T(8,128)(2,1)S(1)}, u32[]{:S(2)}, u32[]{:S(2)}) collective-permute-start(f16[256,256]{1,0:T(8,128)(2,1)S(1)} %multiply_convert_fusion.1), channel_id=1, source_target_pairs={{0,1},{1,0},{2,3},{3,2},{4,5},{5,4},{6,7},{7,6},{8,9},{9,8},{10,11... | collective-permute-start | bytes 393224 | tf_op jit(solution)/shard_map/ppermute | solution.py:449
  4.1 1.0 %collective-permute-done = f16[256,256]{1,0:T(8,128)(2,1)S(1)} collective-permute-done((f16[256,256]{1,0:T(8,128)(2,1)S(1)}, f16[256,256]{1,0:T(8,128)(2,1)S(1)}, u32[]{:S(2)}, u32[]{:S(2)}) %collective-permute-start) | collective-permute-done | bytes 131104 | tf_op jit(solution)/shard_map/ppermute | solution.py:449
  5.1 0.1 multiply_convert_fusion
  5.2 0.5 %collective-permute-start.1 = (f16[256,256]{1,0:T(8,128)(2,1)S(1)}, f16[256,256]{1,0:T(8,128)(2,1)S(1)}, u32[]{:S(2)}, u32[]{:S(2)}) collective-permute-start(f16[256,256]{1,0:T(8,128)(2,1)S(1)} %get-tuple-element.19), channel_id=1, source_target_pairs={{0,2},{3,6},{7,10},{11,14},{15,12},{13,8},{9,4},{5,1},{2,0},{6,3},... | collective-permute-start | bytes 393224 | tf_op jit(solution)/shard_map/ppermute | solution.py:456
  5.7 1.3 %collective-permute-start.3 = (f16[256,256]{1,0:T(8,128)(2,1)S(1)}, f16[256,256]{1,0:T(8,128)(2,1)S(1)}, u32[]{:S(2)}, u32[]{:S(2)}) collective-permute-start(f16[256,256]{1,0:T(8,128)(2,1)S(1)} %get-tuple-element.19), channel_id=1, source_target_pairs={{0,6},{7,4},{5,1},{14,8},{9,10},{11,15},{2,3},{12,13},{6,0},{4,7},... | collective-permute-start | bytes 393224 | tf_op jit(solution)/shard_map/ppermute | solution.py:456
  6.9 0.9 %collective-permute-start.4 = (f16[256,256]{1,0:T(8,128)(2,1)S(1)}, f16[256,256]{1,0:T(8,128)(2,1)S(1)}, u32[]{:S(2)}, u32[]{:S(2)}) collective-permute-start(f16[256,256]{1,0:T(8,128)(2,1)S(1)} %get-tuple-element.19), channel_id=1, source_target_pairs={{2,4},{5,10},{11,12},{13,6},{7,8},{9,3},{0,1},{14,15},{4,2},{10,5}... | collective-permute-start | bytes 393224 | tf_op jit(solution)/shard_map/ppermute | solution.py:456
  7.8 2.1 %spectral_part.3.refs_3_ = f32[2048,256]{1,0:T(8,128)S(1)} custom-call(f32[256,256]{1,0:T(8,128)S(1)} %get-tuple-element.20.refs_0_, f32[7,2,64,32,128]{4,3,2,1,0:T(8,128)} %refs_3_.1, bf16[1024,256]{1,0:T(8,128)(2,1)S(1)} %get-tuple-element.13.refs_2_.refs_3_.refs_4_), custom_call_target="tpu_custom_call" | custom-call | flops 402653184 | bytes 2097152 | tf_op jit(solution)/shard_map/spectral_part/pallas_call | solution.py:366
  9.9 0.0 collective-permute-done.1
  10.0 0.8 %collective-permute-start.2 = (f16[256,256]{1,0:T(8,128)(2,1)S(1)}, f16[256,256]{1,0:T(8,128)(2,1)S(1)}, u32[]{:S(2)}, u32[]{:S(2)}) collective-permute-start(f16[256,256]{1,0:T(8,128)(2,1)S(1)} %collective-permute-done.1), channel_id=1, source_target_pairs={{0,1},{1,0},{2,3},{3,2},{4,5},{5,4},{6,7},{7,6},{8,9},{9,8},{10,11... | collective-permute-start | bytes 393224 | tf_op jit(solution)/shard_map/ppermute | solution.py:467
  10.8 2.3 %spectral_part.4.refs_4_ = f32[2048,256]{1,0:T(8,128)S(1)} custom-call(f32[256,256]{1,0:T(8,128)S(1)} %convert_multiply_fusion.4.refs_0_, f32[7,2,64,32,128]{4,3,2,1,0:T(8,128)} %refs_3_.1, bf16[1024,256]{1,0:T(8,128)(2,1)S(1)} %get-tuple-element.13.refs_2_.refs_3_.refs_4_, f32[2048,256]{1,0:T(8,128)S(1)} %spectral_part.3.refs_3_), custom_call_target="tpu_custom_call" | custom-call | flops 402653184 | bytes 2097152 | tf_op jit(solution)/shard_map/spectral_part/pallas_call | solution.py:366
  13.1 0.0 collective-permute-done.3
  13.1 0.6 %collective-permute-done.4 = f16[256,256]{1,0:T(8,128)(2,1)S(1)} collective-permute-done((f16[256,256]{1,0:T(8,128)(2,1)S(1)}, f16[256,256]{1,0:T(8,128)(2,1)S(1)}, u32[]{:S(2)}, u32[]{:S(2)}) %collective-permute-start.4) | collective-permute-done | bytes 131104 | tf_op jit(solution)/shard_map/ppermute | solution.py:456
  13.8 0.1 pad_maximum_fusion
  13.9 2.4 %collective-permute-start.5 = (f16[512,256]{1,0:T(8,128)(2,1)S(1)}, f16[512,256]{1,0:T(8,128)(2,1)S(1)}, u32[]{:S(2)}, u32[]{:S(2)}) collective-permute-start(f16[512,256]{1,0:T(8,128)(2,1)S(1)} %pad_maximum_fusion), channel_id=1, source_target_pairs={{0,1},{1,0},{2,3},{3,2},{4,5},{5,4},{6,7},{7,6},{8,9},{9,8},{10,11... | collective-permute-start | bytes 786440 | tf_op jit(solution)/shard_map/ppermute | solution.py:467
  16.3 3.8 %spectral_part.5.refs_5_ = f32[2048,256]{1,0:T(8,128)S(1)} custom-call(f32[256,256]{1,0:T(8,128)S(1)} %get-tuple-element.24.refs_0_, f32[256,256]{1,0:T(8,128)S(1)} %get-tuple-element.23.refs_1_, f32[7,2,64,32,128]{4,3,2,1,0:T(8,128)} %refs_3_.1, bf16[1024,256]{1,0:T(8,128)(2,1)S(1)} %get-tuple-element.13.refs_2_.refs_3_.refs_4_, ...), custom_call_target="tpu_custom_call" | custom-call | flops 805306368 | bytes 4194304 | tf_op jit(solution)/shard_map/spectral_part/pallas_call | solution.py:366
  20.1 0.0 collective-permute-done.2
  20.1 0.0 collective-permute-done.5
  20.2 0.0 copy-start
  20.2 6.8 %spectral_last.1.own_ref = f32[512,128]{1,0:T(8,128)S(1)} custom-call(f32[256,256]{1,0:T(8,128)S(1)} %convert_multiply_fusion.5.refs_0_, f32[256,256]{1,0:T(8,128)S(1)} %get-tuple-element.22.refs_1_, f32[256,256]{1,0:T(8,128)S(1)} %get-tuple-element.21.refs_2_, f32[7,2,64,32,128]{4,3,2,1,0:T(8,128)} %refs_3_.1, ...), custom_call_target="tpu_custom_call" | custom-call | flops 1207959552 | bytes 6291456 | tf_op jit(solution)/shard_map/spectral_last/pallas_call | solution.py:366
  26.9 0.1 collective-permute-start.6
  27.0 1.5 %collective-permute-done.6.other_ref = f32[512,128]{1,0:T(8,128)S(1)} collective-permute-done((f32[512,128]{1,0:T(8,128)S(1)}, f32[512,128]{1,0:T(8,128)S(1)}, u32[]{:S(2)}, u32[]{:S(2)}) %collective-permute-start.6) | collective-permute-done | bytes 262176 | tf_op jit(solution)/shard_map/ppermute | solution.py:477
  28.6 0.0 copy-done
  28.6 8.6 %gather.1 = f32[3,1,16384]{2,1,0:T(1,128)} custom-call(f32[512,128]{1,0:T(8,128)S(1)} %spectral_last.1.own_ref, f32[512,128]{1,0:T(8,128)S(1)} %collective-permute-done.6.other_ref, s32[1,16384]{1,0:T(1,128)S(1)} %copy-done), custom_call_target="tpu_custom_call" | custom-call | tf_op jit(solution)/shard_map/gather/pallas_call | solution.py:427
  (5 shorter events, 0.2 us)
Async XLA Ops:
  3.4 1.7 %collective-permute-start = (f16[256,256]{1,0:T(8,128)(2,1)S(1)}, f16[256,256]{1,0:T(8,128)(2,1)S(1)}, u32[]{:S(2)}, u32[]{:S(2)}) collective-permute-start(f16[256,256]{1,0:T(8,128)(2,1)S(1)} %multiply_convert_fusion.1), channel_id=1, source_target_pairs={{0,1},{1,0},{2,3},{3,2},{4,5},{5,4},{6,7},{7,6},{8,9},{9,8},{10,11... | collective-permute-start | bytes 393224 | tf_op jit(solution)/shard_map/ppermute | solution.py:449
  5.2 4.8 %collective-permute-start.1 = (f16[256,256]{1,0:T(8,128)(2,1)S(1)}, f16[256,256]{1,0:T(8,128)(2,1)S(1)}, u32[]{:S(2)}, u32[]{:S(2)}) collective-permute-start(f16[256,256]{1,0:T(8,128)(2,1)S(1)} %get-tuple-element.19), channel_id=1, source_target_pairs={{0,2},{3,6},{7,10},{11,14},{15,12},{13,8},{9,4},{5,1},{2,0},{6,3},... | collective-permute-start | bytes 393224 | tf_op jit(solution)/shard_map/ppermute | solution.py:456
  5.7 7.5 %collective-permute-start.3 = (f16[256,256]{1,0:T(8,128)(2,1)S(1)}, f16[256,256]{1,0:T(8,128)(2,1)S(1)}, u32[]{:S(2)}, u32[]{:S(2)}) collective-permute-start(f16[256,256]{1,0:T(8,128)(2,1)S(1)} %get-tuple-element.19), channel_id=1, source_target_pairs={{0,6},{7,4},{5,1},{14,8},{9,10},{11,15},{2,3},{12,13},{6,0},{4,7},... | collective-permute-start | bytes 393224 | tf_op jit(solution)/shard_map/ppermute | solution.py:456
  6.9 6.8 %collective-permute-start.4 = (f16[256,256]{1,0:T(8,128)(2,1)S(1)}, f16[256,256]{1,0:T(8,128)(2,1)S(1)}, u32[]{:S(2)}, u32[]{:S(2)}) collective-permute-start(f16[256,256]{1,0:T(8,128)(2,1)S(1)} %get-tuple-element.19), channel_id=1, source_target_pairs={{2,4},{5,10},{11,12},{13,6},{7,8},{9,3},{0,1},{14,15},{4,2},{10,5}... | collective-permute-start | bytes 393224 | tf_op jit(solution)/shard_map/ppermute | solution.py:456
  10.0 10.1 %collective-permute-start.2 = (f16[256,256]{1,0:T(8,128)(2,1)S(1)}, f16[256,256]{1,0:T(8,128)(2,1)S(1)}, u32[]{:S(2)}, u32[]{:S(2)}) collective-permute-start(f16[256,256]{1,0:T(8,128)(2,1)S(1)} %collective-permute-done.1), channel_id=1, source_target_pairs={{0,1},{1,0},{2,3},{3,2},{4,5},{5,4},{6,7},{7,6},{8,9},{9,8},{10,11... | collective-permute-start | bytes 393224 | tf_op jit(solution)/shard_map/ppermute | solution.py:467
  13.9 6.2 %collective-permute-start.5 = (f16[512,256]{1,0:T(8,128)(2,1)S(1)}, f16[512,256]{1,0:T(8,128)(2,1)S(1)}, u32[]{:S(2)}, u32[]{:S(2)}) collective-permute-start(f16[512,256]{1,0:T(8,128)(2,1)S(1)} %pad_maximum_fusion), channel_id=1, source_target_pairs={{0,1},{1,0},{2,3},{3,2},{4,5},{5,4},{6,7},{7,6},{8,9},{9,8},{10,11... | collective-permute-start | bytes 786440 | tf_op jit(solution)/shard_map/ppermute | solution.py:467
  20.2 8.4 %copy-start = (s32[1,16384]{1,0:T(1,128)S(1)}, s32[1,16384]{1,0:T(1,128)}, u32[]{:S(2)}) copy-start(s32[1,16384]{1,0:T(1,128)} %cell_ref.1) | copy-start | bytes 196612
  26.9 1.6 %collective-permute-start.6 = (f32[512,128]{1,0:T(8,128)S(1)}, f32[512,128]{1,0:T(8,128)S(1)}, u32[]{:S(2)}, u32[]{:S(2)}) collective-permute-start(f32[512,128]{1,0:T(8,128)S(1)} %spectral_last.1.own_ref), channel_id=1, source_target_pairs={{0,1},{1,0},{2,3},{3,2},{4,5},{5,4},{6,7},{7,6},{8,9},{9,8},{10,11... | collective-permute-start | bytes 786440 | tf_op jit(solution)/shard_map/ppermute | solution.py:477

commit v7 on v6

--- a/solution.py
+++ b/solution.py
@@ -219,9 +219,9 @@
         lanes = slice(low * GZ, (low + 1) * GZ)
         terms = jnp.concatenate([top[:, lanes], rest[:, lanes], top[:, lanes]], axis=1)
         after_z[:, 2 * MZ * low : 2 * MZ * (low + 1)] = dot(terms, table_z)
-    for pair in range(GY // 2):
+    for group in range(GY // 4):
         sides = []
-        for y in (2 * pair, 2 * pair + 1):
+        for y in range(4 * group, 4 * group + 4):
             tiles = [
                 after_z[8 * y : 8 * y + 8, (2 * low + part) * MZ : (2 * low + part + 1) * MZ]
                 for part in range(2)
@@ -229,8 +229,8 @@
             ]
             sides.append(jnp.concatenate(tiles, axis=0))
         out = dot(table_x, data_terms(jnp.concatenate(sides, axis=1)))
-        for side in range(2):
-            rows = pl.ds((2 * pair + side) * PITCH_X, 2 * MX)
+        for side in range(4):
+            rows = pl.ds((4 * group + side) * PITCH_X, 2 * MX)
             after_x[at, rows, :] = out[:, side * MZ : (side + 1) * MZ]
 
 

time: 37.3 us -> 37.3 us (level)
  no operation moved by 1% of the time
where the time goes in v7:
time: 37.3 us; the launch traced here: 37.1 us
  Pallas kernels  25.9 us (69%)
  starting transfers between devices  6.69 us (18%)
  waiting for transfers between devices  3.12 us (8%)
  other arithmetic  1.27 us (3%)
    pallas_call x4, Pallas kernels, spectral(): pl.pallas_call(functools.partial(spectral_kernel, places, offsets, first,...  15 us
    pallas_call x1, Pallas kernels, gather(): pl.pallas_call(gather_kernel, out_shape=jax.ShapeDtypeStruct((3, 1, cells...  8.57 us
    ppermute x2, starting transfers between devices, per_device(): beyond = lax.ppermute(jnp.concatenate(arrivals), 'pencil', swap)  3.26 us
    ppermute x3, starting transfers between devices, per_device(): near.append(lax.ppermute(sent, ('bunch', 'pencil'), route))  2.62 us
    pallas_call x1, Pallas kernels, deposit(): pl.pallas_call(deposit_kernel, in_specs=[pl.BlockSpec(memory_space=pltpu....  2.38 us
    ppermute x1, waiting for transfers between devices, per_device(): other = lax.ppermute(own, 'pencil', swap)  1.52 us
    ppermute x1, waiting for transfers between devices, per_device(): density = part + received(lax.ppermute(partial, 'pencil', swap))  0.99 us
    add x1, other arithmetic, deposit(): particles = (cells << CHARGE_BITS) + units  0.98 us
  transfers between devices with their start and end apart: 7, of which 3 were waited for; matrix products, arithmetic and copies ran while one was open for 0% of the time, Pallas kernels for 22%

profile of v7, /device:TPU:17, one launch (start us, length us, event | category | flops | bytes accessed | tf_op | source)
XLA Modules:
  0.0 37.1 jit_solution(16780582310150413050)
XLA Ops:
  0.0 1.0 %convert_add_fusion.particles_ref = s32[1,16384]{1,0:T(1,128)S(1)} fusion(bf16[1,16384]{1,0:T(2,128)(2,1)} %param.5, s32[1,16384]{1,0:T(1,128)} %param.6), kind=kLoop, calls=%fused_computation.10 | loop fusion | flops 81920 | bytes 163840 | tf_op jit(solution)/shard_map/add | solution.py:191
  1.0 2.4 %deposit.1 = (f32[256,256]{1,0:T(8,128)S(1)}, bf16[1024,256]{1,0:T(8,128)(2,1)S(1)}) custom-call(s32[1,16384]{1,0:T(1,128)S(1)} %convert_add_fusion.particles_ref, bf16[1024,256]{1,0:T(8,128)(2,1)} %constant.10.clone.table_hbm), custom_call_target="tpu_custom_call" | custom-call | tf_op jit(solution)/shard_map/deposit/pallas_call | solution.py:192
  3.4 0.7 %collective-permute-start = (f16[256,256]{1,0:T(8,128)(2,1)S(1)}, f16[256,256]{1,0:T(8,128)(2,1)S(1)}, u32[]{:S(2)}, u32[]{:S(2)}) collective-permute-start(f16[256,256]{1,0:T(8,128)(2,1)S(1)} %multiply_convert_fusion.1), channel_id=1, source_target_pairs={{0,1},{1,0},{2,3},{3,2},{4,5},{5,4},{6,7},{7,6},{8,9},{9,8},{10,11... | collective-permute-start | bytes 393224 | tf_op jit(solution)/shard_map/ppermute | solution.py:449
  4.1 1.0 %collective-permute-done = f16[256,256]{1,0:T(8,128)(2,1)S(1)} collective-permute-done((f16[256,256]{1,0:T(8,128)(2,1)S(1)}, f16[256,256]{1,0:T(8,128)(2,1)S(1)}, u32[]{:S(2)}, u32[]{:S(2)}) %collective-permute-start) | collective-permute-done | bytes 131104 | tf_op jit(solution)/shard_map/ppermute | solution.py:449
  5.1 0.1 multiply_convert_fusion
  5.2 0.5 %collective-permute-start.1 = (f16[256,256]{1,0:T(8,128)(2,1)S(1)}, f16[256,256]{1,0:T(8,128)(2,1)S(1)}, u32[]{:S(2)}, u32[]{:S(2)}) collective-permute-start(f16[256,256]{1,0:T(8,128)(2,1)S(1)} %get-tuple-element.19), channel_id=1, source_target_pairs={{0,2},{3,6},{7,10},{11,14},{15,12},{13,8},{9,4},{5,1},{2,0},{6,3},... | collective-permute-start | bytes 393224 | tf_op jit(solution)/shard_map/ppermute | solution.py:456
  5.7 1.3 %collective-permute-start.3 = (f16[256,256]{1,0:T(8,128)(2,1)S(1)}, f16[256,256]{1,0:T(8,128)(2,1)S(1)}, u32[]{:S(2)}, u32[]{:S(2)}) collective-permute-start(f16[256,256]{1,0:T(8,128)(2,1)S(1)} %get-tuple-element.19), channel_id=1, source_target_pairs={{0,6},{7,4},{5,1},{14,8},{9,10},{11,15},{2,3},{12,13},{6,0},{4,7},... | collective-permute-start | bytes 393224 | tf_op jit(solution)/shard_map/ppermute | solution.py:456
  6.9 0.9 %collective-permute-start.4 = (f16[256,256]{1,0:T(8,128)(2,1)S(1)}, f16[256,256]{1,0:T(8,128)(2,1)S(1)}, u32[]{:S(2)}, u32[]{:S(2)}) collective-permute-start(f16[256,256]{1,0:T(8,128)(2,1)S(1)} %get-tuple-element.19), channel_id=1, source_target_pairs={{2,4},{5,10},{11,12},{13,6},{7,8},{9,3},{0,1},{14,15},{4,2},{10,5}... | collective-permute-start | bytes 393224 | tf_op jit(solution)/shard_map/ppermute | solution.py:456
  7.8 2.1 %spectral_part.3.refs_3_ = f32[2048,256]{1,0:T(8,128)S(1)} custom-call(f32[256,256]{1,0:T(8,128)S(1)} %get-tuple-element.20.refs_0_, f32[7,2,64,32,128]{4,3,2,1,0:T(8,128)} %refs_3_.1, bf16[1024,256]{1,0:T(8,128)(2,1)S(1)} %get-tuple-element.13.refs_2_.refs_3_.refs_4_), custom_call_target="tpu_custom_call" | custom-call | flops 402653184 | bytes 2097152 | tf_op jit(solution)/shard_map/spectral_part/pallas_call | solution.py:366
  9.9 0.0 collective-permute-done.1
  10.0 0.8 %collective-permute-start.2 = (f16[256,256]{1,0:T(8,128)(2,1)S(1)}, f16[256,256]{1,0:T(8,128)(2,1)S(1)}, u32[]{:S(2)}, u32[]{:S(2)}) collective-permute-start(f16[256,256]{1,0:T(8,128)(2,1)S(1)} %collective-permute-done.1), channel_id=1, source_target_pairs={{0,1},{1,0},{2,3},{3,2},{4,5},{5,4},{6,7},{7,6},{8,9},{9,8},{10,11... | collective-permute-start | bytes 393224 | tf_op jit(solution)/shard_map/ppermute | solution.py:467
  10.8 2.3 %spectral_part.4.refs_4_ = f32[2048,256]{1,0:T(8,128)S(1)} custom-call(f32[256,256]{1,0:T(8,128)S(1)} %convert_multiply_fusion.4.refs_0_, f32[7,2,64,32,128]{4,3,2,1,0:T(8,128)} %refs_3_.1, bf16[1024,256]{1,0:T(8,128)(2,1)S(1)} %get-tuple-element.13.refs_2_.refs_3_.refs_4_, f32[2048,256]{1,0:T(8,128)S(1)} %spectral_part.3.refs_3_), custom_call_target="tpu_custom_call" | custom-call | flops 402653184 | bytes 2097152 | tf_op jit(solution)/shard_map/spectral_part/pallas_call | solution.py:366
  13.1 0.0 collective-permute-done.3
  13.1 0.6 %collective-permute-done.4 = f16[256,256]{1,0:T(8,128)(2,1)S(1)} collective-permute-done((f16[256,256]{1,0:T(8,128)(2,1)S(1)}, f16[256,256]{1,0:T(8,128)(2,1)S(1)}, u32[]{:S(2)}, u32[]{:S(2)}) %collective-permute-start.4) | collective-permute-done | bytes 131104 | tf_op jit(solution)/shard_map/ppermute | solution.py:456
  13.8 0.1 pad_maximum_fusion
  13.9 2.4 %collective-permute-start.5 = (f16[512,256]{1,0:T(8,128)(2,1)S(1)}, f16[512,256]{1,0:T(8,128)(2,1)S(1)}, u32[]{:S(2)}, u32[]{:S(2)}) collective-permute-start(f16[512,256]{1,0:T(8,128)(2,1)S(1)} %pad_maximum_fusion), channel_id=1, source_target_pairs={{0,1},{1,0},{2,3},{3,2},{4,5},{5,4},{6,7},{7,6},{8,9},{9,8},{10,11... | collective-permute-start | bytes 786440 | tf_op jit(solution)/shard_map/ppermute | solution.py:467
  16.3 3.8 %spectral_part.5.refs_5_ = f32[2048,256]{1,0:T(8,128)S(1)} custom-call(f32[256,256]{1,0:T(8,128)S(1)} %get-tuple-element.24.refs_0_, f32[256,256]{1,0:T(8,128)S(1)} %get-tuple-element.23.refs_1_, f32[7,2,64,32,128]{4,3,2,1,0:T(8,128)} %refs_3_.1, bf16[1024,256]{1,0:T(8,128)(2,1)S(1)} %get-tuple-element.13.refs_2_.refs_3_.refs_4_, ...), custom_call_target="tpu_custom_call" | custom-call | flops 805306368 | bytes 4194304 | tf_op jit(solution)/shard_map/spectral_part/pallas_call | solution.py:366
  20.1 0.0 collective-permute-done.2
  20.1 0.0 collective-permute-done.5
  20.2 0.0 copy-start
  20.2 6.8 %spectral_last.1.own_ref = f32[512,128]{1,0:T(8,128)S(1)} custom-call(f32[256,256]{1,0:T(8,128)S(1)} %convert_multiply_fusion.5.refs_0_, f32[256,256]{1,0:T(8,128)S(1)} %get-tuple-element.22.refs_1_, f32[256,256]{1,0:T(8,128)S(1)} %get-tuple-element.21.refs_2_, f32[7,2,64,32,128]{4,3,2,1,0:T(8,128)} %refs_3_.1, ...), custom_call_target="tpu_custom_call" | custom-call | flops 1207959552 | bytes 6291456 | tf_op jit(solution)/shard_map/spectral_last/pallas_call | solution.py:366
  26.9 0.1 collective-permute-start.6
  27.0 1.5 %collective-permute-done.6.other_ref = f32[512,128]{1,0:T(8,128)S(1)} collective-permute-done((f32[512,128]{1,0:T(8,128)S(1)}, f32[512,128]{1,0:T(8,128)S(1)}, u32[]{:S(2)}, u32[]{:S(2)}) %collective-permute-start.6) | collective-permute-done | bytes 262176 | tf_op jit(solution)/shard_map/ppermute | solution.py:477
  28.6 0.0 copy-done
  28.6 8.6 %gather.1 = f32[3,1,16384]{2,1,0:T(1,128)} custom-call(f32[512,128]{1,0:T(8,128)S(1)} %spectral_last.1.own_ref, f32[512,128]{1,0:T(8,128)S(1)} %collective-permute-done.6.other_ref, s32[1,16384]{1,0:T(1,128)S(1)} %copy-done), custom_call_target="tpu_custom_call" | custom-call | tf_op jit(solution)/shard_map/gather/pallas_call | solution.py:427
  (5 shorter events, 0.2 us)
Async XLA Ops:
  3.4 1.7 %collective-permute-start = (f16[256,256]{1,0:T(8,128)(2,1)S(1)}, f16[256,256]{1,0:T(8,128)(2,1)S(1)}, u32[]{:S(2)}, u32[]{:S(2)}) collective-permute-start(f16[256,256]{1,0:T(8,128)(2,1)S(1)} %multiply_convert_fusion.1), channel_id=1, source_target_pairs={{0,1},{1,0},{2,3},{3,2},{4,5},{5,4},{6,7},{7,6},{8,9},{9,8},{10,11... | collective-permute-start | bytes 393224 | tf_op jit(solution)/shard_map/ppermute | solution.py:449
  5.2 4.8 %collective-permute-start.1 = (f16[256,256]{1,0:T(8,128)(2,1)S(1)}, f16[256,256]{1,0:T(8,128)(2,1)S(1)}, u32[]{:S(2)}, u32[]{:S(2)}) collective-permute-start(f16[256,256]{1,0:T(8,128)(2,1)S(1)} %get-tuple-element.19), channel_id=1, source_target_pairs={{0,2},{3,6},{7,10},{11,14},{15,12},{13,8},{9,4},{5,1},{2,0},{6,3},... | collective-permute-start | bytes 393224 | tf_op jit(solution)/shard_map/ppermute | solution.py:456
  5.7 7.5 %collective-permute-start.3 = (f16[256,256]{1,0:T(8,128)(2,1)S(1)}, f16[256,256]{1,0:T(8,128)(2,1)S(1)}, u32[]{:S(2)}, u32[]{:S(2)}) collective-permute-start(f16[256,256]{1,0:T(8,128)(2,1)S(1)} %get-tuple-element.19), channel_id=1, source_target_pairs={{0,6},{7,4},{5,1},{14,8},{9,10},{11,15},{2,3},{12,13},{6,0},{4,7},... | collective-permute-start | bytes 393224 | tf_op jit(solution)/shard_map/ppermute | solution.py:456
  6.9 6.8 %collective-permute-start.4 = (f16[256,256]{1,0:T(8,128)(2,1)S(1)}, f16[256,256]{1,0:T(8,128)(2,1)S(1)}, u32[]{:S(2)}, u32[]{:S(2)}) collective-permute-start(f16[256,256]{1,0:T(8,128)(2,1)S(1)} %get-tuple-element.19), channel_id=1, source_target_pairs={{2,4},{5,10},{11,12},{13,6},{7,8},{9,3},{0,1},{14,15},{4,2},{10,5}... | collective-permute-start | bytes 393224 | tf_op jit(solution)/shard_map/ppermute | solution.py:456
  10.0 10.1 %collective-permute-start.2 = (f16[256,256]{1,0:T(8,128)(2,1)S(1)}, f16[256,256]{1,0:T(8,128)(2,1)S(1)}, u32[]{:S(2)}, u32[]{:S(2)}) collective-permute-start(f16[256,256]{1,0:T(8,128)(2,1)S(1)} %collective-permute-done.1), channel_id=1, source_target_pairs={{0,1},{1,0},{2,3},{3,2},{4,5},{5,4},{6,7},{7,6},{8,9},{9,8},{10,11... | collective-permute-start | bytes 393224 | tf_op jit(solution)/shard_map/ppermute | solution.py:467
  13.9 6.2 %collective-permute-start.5 = (f16[512,256]{1,0:T(8,128)(2,1)S(1)}, f16[512,256]{1,0:T(8,128)(2,1)S(1)}, u32[]{:S(2)}, u32[]{:S(2)}) collective-permute-start(f16[512,256]{1,0:T(8,128)(2,1)S(1)} %pad_maximum_fusion), channel_id=1, source_target_pairs={{0,1},{1,0},{2,3},{3,2},{4,5},{5,4},{6,7},{7,6},{8,9},{9,8},{10,11... | collective-permute-start | bytes 786440 | tf_op jit(solution)/shard_map/ppermute | solution.py:467
  20.2 8.4 %copy-start = (s32[1,16384]{1,0:T(1,128)S(1)}, s32[1,16384]{1,0:T(1,128)}, u32[]{:S(2)}) copy-start(s32[1,16384]{1,0:T(1,128)} %cell_ref.1) | copy-start | bytes 196612
  26.9 1.6 %collective-permute-start.6 = (f32[512,128]{1,0:T(8,128)S(1)}, f32[512,128]{1,0:T(8,128)S(1)}, u32[]{:S(2)}, u32[]{:S(2)}) collective-permute-start(f32[512,128]{1,0:T(8,128)S(1)} %spectral_last.1.own_ref), channel_id=1, source_target_pairs={{0,1},{1,0},{2,3},{3,2},{4,5},{5,4},{6,7},{7,6},{8,9},{9,8},{10,11... | collective-permute-start | bytes 786440 | tf_op jit(solution)/shard_map/ppermute | solution.py:477
